TPU v7x, 32 devices: a whole 2x2x4 slice. The times are simulated.
32 devices in a mesh: groups: 2 (over y), expert: 4 (over z), dp: 2 (over x), pair: 2 (over core).
Axes of the slice: x: 2, y: 2, z: 4, core: 2. Of those that a mesh axis runs over, the one named last changes fastest.
Arguments:
- out_grad: bfloat16 [4, 128, 4096], P(('groups', 'dp'), ('expert', 'pair')), parts along dimension 0, may hold values from -6 to 6
- merged: bfloat16 [4, 128, 4096], P(('groups', 'dp'), None, ('expert', 'pair')), parts along dimension 0, may hold values from -6 to 6
- sub_tokens: bfloat16 [4, 128, 4, 1024], P(('groups', 'dp'), ('expert', 'pair')), parts along dimension 0, may hold values from -6 to 6
- routes: int32 [4, 128, 4, 2], P(('groups', 'dp'), ('expert', 'pair')), parts along dimension 0, may hold values from 0 to 7, all different within a row; in each aligned block of 64 rows (0 to 63, 64 to 127, ..., all dimensions but the last counted through in order) at most 24 rows name the same one
- gate_probs: bfloat16 [4, 128, 4, 2], P(('groups', 'dp'), ('expert', 'pair')), parts along dimension 0, may hold values from 0.049804688 to 1
- merge_weight: bfloat16 [4096, 4096], P(('expert', 'pair'), 'dp'), may hold values from -0.09375 to 0.09375
- expert_in: bfloat16 [8, 1024, 1024], P(('expert', 'dp'), None, 'pair'), may hold values from -0.1875 to 0.1875
- expert_out: bfloat16 [8, 1024, 1024], P(('expert', 'dp'), 'pair'), may hold values from -0.1875 to 0.1875
Outputs:
- merge_grad: bfloat16 [8192, 4096], P(('groups', 'expert', 'pair'), 'dp'), parts along dimension 0
- grad_sub: bfloat16 [4, 128, 4, 1024], P(('groups', 'dp'), ('expert', 'pair')), parts along dimension 0
- grad_probs: bfloat16 [4, 128, 4, 2], P(('groups', 'dp'), ('expert', 'pair')), parts along dimension 0
- grad_in: bfloat16 [16, 1024, 1024], P(('groups', 'expert', 'dp'), None, 'pair'), parts along dimension 0
- grad_out: bfloat16 [16, 1024, 1024], P(('groups', 'expert', 'dp'), 'pair'), parts along dimension 0
There are 2 independent parts, one for each index of `groups`. A program takes and returns all parts, laid end to end along the dimension named above; an argument that names none is the same for every part. Nothing has to cross between parts.
Inputs may be any that keep to these rules, and one draw needn't show every extreme that they name: `routes`: each sub-token names 2 different experts; the sub-tokens of one device name one expert at most 24 times.
All inputs are finite; a program needn't handle non-finite values.
Results may differ from a plain program's by a relative error of at most 0.0072.
Values may be sent and summed in bfloat16 or wider, within the bound.
A program may use at most 64 MiB of HBM per device.

v0:
```python
import jax
import jax.numpy as jnp
from jax import lax
from jax.sharding import PartitionSpec as P


def expert_block(inputs, head_part, gates, first, second):
    preact = jnp.dot(inputs, first, preferred_element_type=jnp.float32)
    activated, pullback = jax.vjp(jax.nn.gelu, preact)
    back_hidden = lax.dot_general(
        head_part, second, (((1,), (1,)), ((), ())), preferred_element_type=jnp.float32
    )
    prob_half = jnp.sum(activated * back_hidden, axis=1)
    scales = gates.astype(jnp.float32)[:, None]
    hidden_grad = pullback(scales * back_hidden)[0].astype(jnp.bfloat16)
    out_scaled = (scales * head_part.astype(jnp.float32)).astype(jnp.bfloat16)
    act_low = activated.astype(jnp.bfloat16)
    grad_first = lax.dot_general(
        inputs, hidden_grad, (((0,), (0,)), ((), ())), preferred_element_type=jnp.float32
    )
    grad_second = lax.dot_general(
        act_low, out_scaled, (((0,), (0,)), ((), ())), preferred_element_type=jnp.float32
    )
    input_half = lax.dot_general(
        hidden_grad, first, (((1,), (1,)), ((), ())), preferred_element_type=jnp.float32
    )
    return (input_half, prob_half, grad_first, grad_second)


def per_device(
    out_grad, merged, sub_tokens, routes, gate_probs, merge_weight, expert_in, expert_out
):
    expert_size = lax.axis_size("expert")
    data_size = lax.axis_size("dp")
    experts = expert_size * data_size
    saved = merged[0]
    weight_rows = lax.all_gather(merge_weight, "dp", axis=1, tiled=True)
    tokens_here = lax.all_gather(out_grad, ("expert", "pair"), axis=1, tiled=True)[0]
    local = lax.dot_general(
        tokens_here, weight_rows, (((1,), (1,)), ((), ())), preferred_element_type=jnp.float32
    ).astype(jnp.bfloat16)
    head_block = local
    partial_value = lax.dot_general(
        saved, tokens_here, (((0,), (0,)), ((), ())), preferred_element_type=jnp.float32
    )
    head_block, partial_value = (head_block, partial_value)
    merge_grad = lax.psum_scatter(partial_value, "dp", scatter_dimension=1, tiled=True).astype(
        jnp.bfloat16
    )
    head_grad = lax.all_to_all(
        head_block, ("expert", "pair"), split_axis=0, concat_axis=1, tiled=True
    )
    positions = sub_tokens.shape[1]
    head_count = sub_tokens.shape[2]
    head_dim = sub_tokens.shape[3]
    top_count = routes.shape[3]
    routed_count = positions * head_count * top_count
    capacity = max(2, 3 * routed_count // (2 * experts))
    flat_ids = routes[0].reshape(routed_count)
    onehot = (flat_ids[:, None] == jnp.arange(experts, dtype=jnp.int32)[None, :]).astype(jnp.int32)
    slot_rank = jnp.sum((jnp.cumsum(onehot, axis=0) - onehot) * onehot, axis=1)
    shape_rows = (positions, head_count, top_count, head_dim)
    flat_inputs = jnp.broadcast_to(sub_tokens[0][:, :, None, :], shape_rows).reshape(
        routed_count, head_dim
    )
    flat_heads = jnp.broadcast_to(
        head_grad.reshape(positions, head_count, 1, head_dim), shape_rows
    ).reshape(routed_count, head_dim)
    flat_gates = gate_probs[0].reshape(routed_count)
    send_inputs = (
        jnp.zeros((experts, capacity, head_dim), jnp.bfloat16)
        .at[flat_ids, slot_rank]
        .set(flat_inputs)
    )
    send_heads = (
        jnp.zeros((experts, capacity, head_dim), jnp.bfloat16)
        .at[flat_ids, slot_rank]
        .set(flat_heads)
    )
    send_gates = (
        jnp.zeros((experts, capacity), jnp.bfloat16).at[flat_ids, slot_rank].set(flat_gates)
    )
    recv_inputs, recv_heads, recv_gates = (
        lax.all_to_all(send_inputs, ("expert", "dp"), split_axis=0, concat_axis=0, tiled=True),
        lax.all_to_all(send_heads, ("expert", "dp"), split_axis=0, concat_axis=0, tiled=True),
        lax.all_to_all(send_gates, ("expert", "dp"), split_axis=0, concat_axis=0, tiled=True),
    )
    both_inputs, both_heads, both_gates = (
        lax.all_gather(recv_inputs, "pair", axis=0, tiled=True),
        lax.all_gather(recv_heads, "pair", axis=0, tiled=True),
        lax.all_gather(recv_gates, "pair", axis=0, tiled=True),
    )
    slot_count = 2 * experts * capacity
    input_all = both_inputs.reshape(slot_count, head_dim)
    head_all = both_heads.reshape(slot_count, head_dim)
    gate_all = both_gates.reshape(slot_count)
    first = expert_in[0]
    second = expert_out[0]
    half_units = first.shape[1]
    input_part, prob_part, grads_first, grads_second = expert_block(
        input_all, head_all, gate_all, first, second
    )
    input_sum, prob_sum = (
        lax.psum_scatter(
            input_part.reshape(2 * experts, capacity, head_dim).astype(jnp.bfloat16),
            "pair",
            scatter_dimension=0,
            tiled=True,
        ).astype(jnp.float32),
        lax.psum_scatter(
            prob_part.reshape(2 * experts, capacity).astype(jnp.bfloat16),
            "pair",
            scatter_dimension=0,
            tiled=True,
        ).astype(jnp.float32),
    )
    input_low = input_sum.astype(jnp.bfloat16)
    prob_low = prob_sum.astype(jnp.bfloat16)
    back_inputs, back_probs = (
        lax.all_to_all(input_low, ("expert", "dp"), split_axis=0, concat_axis=0, tiled=True),
        lax.all_to_all(prob_low, ("expert", "dp"), split_axis=0, concat_axis=0, tiled=True),
    )
    routed_inputs = (
        back_inputs[flat_ids, slot_rank]
        .astype(jnp.float32)
        .reshape(positions, head_count, top_count, head_dim)
    )
    grad_sub = (
        jnp.sum(routed_inputs, axis=2)
        .astype(jnp.bfloat16)
        .reshape(1, positions, head_count, head_dim)
    )
    grad_probs = back_probs[flat_ids, slot_rank].reshape(1, positions, head_count, top_count)
    grad_in = grads_first.astype(jnp.bfloat16).reshape(1, head_dim, half_units)
    grad_out = grads_second.astype(jnp.bfloat16).reshape(1, half_units, head_dim)
    return (merge_grad, grad_sub, grad_probs, grad_in, grad_out)


def solution(mesh):
    placed = (
        P(("groups", "dp"), ("expert", "pair"), None),
        P(("groups", "dp"), None, ("expert", "pair")),
        P(("groups", "dp"), ("expert", "pair"), None, None),
        P(("groups", "dp"), ("expert", "pair"), None, None),
        P(("groups", "dp"), ("expert", "pair"), None, None),
        P(("expert", "pair"), "dp"),
        P(("expert", "dp"), None, "pair"),
        P(("expert", "dp"), "pair", None),
    )
    return jax.shard_map(
        per_device,
        mesh=mesh,
        in_specs=placed,
        out_specs=(
            P(("groups", "expert", "pair"), "dp"),
            P(("groups", "dp"), ("expert", "pair"), None, None),
            P(("groups", "dp"), ("expert", "pair"), None, None),
            P(("groups", "expert", "dp"), None, "pair"),
            P(("groups", "expert", "dp"), "pair", None),
        ),
        check_vma=False,
    )
```

profile of v0, /device:TPU:0, one launch (start us, length us, event | category | flops | bytes accessed | tf_op | source)
XLA Modules:
  0.0 296.8 jit_solution(2062818022416199146)
XLA Ops:
  7.2 0.0 copy-start
  7.2 0.0 all-gather.4.cloned.1.call-start
  7.2 0.7 all-gather.4.cloned.1.call-update
  7.9 0.0 all-gather.6.cloned.1.call-start
  8.0 0.7 all-gather.6.cloned.1.call-update
  8.7 0.1 copy.36
  8.8 0.1 eq.15
  9.0 0.1 reshape_squeeze.6
  9.1 0.1 copy.38
  9.2 0.1 reshape.131
  9.4 0.1 fusion.20
  9.5 0.2 reduce_window_sum.11
  9.7 0.2 select_reduce_fusion
  9.9 6.5 %scatter_fusion = bf16[8,24]{1,0:T(8,128)(2,1)S(1)} fusion(bf16[8,24]{1,0:T(8,128)(2,1)S(1)} %broadcast_in_dim.10, s32[128]{0:T(128)S(1)} %get-tuple-element.30, bf16[128]{0:T(256)(128)(2,1)S(1)} %reshape.131), kind=kCustom, calls=%fused_computation.2 | custom fusion | bytes 1792 | tf_op jit(solution)/shard_map/scatter | solution.py:81
  16.4 0.6 copy.39
  17.0 7.3 %all-to-all-start = ((bf16[8,1,24]{2,1,0:T(2,128)(2,1)}), bf16[8,1,24]{2,1,0:T(2,128)(2,1)S(1)}, u32[]{:S(2)}, u32[]{:S(2)}) async-start(bf16[8,1,24]{2,1,0:T(2,128)(2,1)} %copy.39), calls=%async_computation.1 | async-start | bytes 8192 | tf_op jit(solution)/shard_map/all_to_all | solution.py:86
  24.2 10.4 %all-gather.4.cloned.1.call-done = bf16[1,128,4096]{2,1,0:T(8,128)(2,1)} async-done(((bf16[1,16,4096]{2,1,0:T(8,128)(2,1)}), bf16[1,128,4096]{2,1,0:T(8,128)(2,1)}) %all-gather.4.cloned.1.call-update) | async-done | bytes 1048592 | tf_op jit(solution)/shard_map/all_gather | solution.py:38
  34.6 57.9 %all-gather.6.cloned.1.call-done = bf16[512,4096]{1,0:T(8,128)(2,1)} async-done(((bf16[512,2048]{1,0:T(8,128)(2,1)}), bf16[512,4096]{1,0:T(8,128)(2,1)}) %all-gather.6.cloned.1.call-update) | async-done | bytes 4194320 | tf_op jit(solution)/shard_map/all_gather | solution.py:37
  92.5 4.7 %convolution_convert_fusion.3 = bf16[128,512]{1,0:T(8,128)(2,1)} fusion(bf16[512,4096]{1,0:T(8,128)(2,1)} %all-gather.6.cloned.1.call-done, bf16[1,128,4096]{2,1,0:T(8,128)(2,1)} %all-gather.4.cloned.1.call-done), kind=kOutput, calls=%fused_computation.11 | convolution fusion | flops 536936448 | bytes 5373952 | tf_op jit(solution)/shard_map/dot_general | solution.py:39
  97.2 4.6 %all-to-all-start.1 = ((bf16[8,16,512]{2,1,0:T(8,128)(2,1)}), bf16[8,16,512]{2,1,0:T(8,128)(2,1)S(1)}, u32[]{:S(2)}, u32[]{:S(2)}) async-start(bf16[8,16,512]{2,1,0:T(8,128)(2,1)} %bitcast.5), calls=%async_computation.2 | async-start | bytes 262144 | tf_op jit(solution)/shard_map/all_to_all | solution.py:50
  101.8 0.2 broadcast_in_dim.14
  102.0 0.1 reshape.143
  102.1 0.8 broadcast.60.clone
  102.9 19.0 %scatter_fusion.2 = bf16[8,24,1024]{2,1,0:T(8,128)(2,1)} fusion(bf16[8,24,1024]{2,1,0:T(8,128)(2,1)} %broadcast.60.clone, s32[128]{0:T(128)S(1)} %get-tuple-element.30, bf16[128,1024]{1,0:T(8,128)(2,1)S(1)} %reshape.143), kind=kCustom, calls=%fused_computation.4 | custom fusion | bytes 787456 | tf_op jit(solution)/shard_map/scatter | solution.py:73
  122.0 5.0 %all-to-all-start.3 = ((bf16[8,24,1024]{2,1,0:T(8,128)(2,1)}), bf16[8,24,1024]{2,1,0:T(8,128)(2,1)S(1)}, u32[]{:S(2)}, u32[]{:S(2)}) async-start(bf16[8,24,1024]{2,1,0:T(8,128)(2,1)} %scatter_fusion.2), calls=%async_computation.4 | async-start | bytes 786432 | tf_op jit(solution)/shard_map/all_to_all | solution.py:84
  126.9 0.1 copy.41
  127.0 0.1 broadcast_in_dim.11
  127.1 0.2 broadcast_in_dim.12
  127.3 0.1 reshape.137
  127.4 0.8 broadcast.60.clone.1
  128.2 19.2 %scatter_fusion.1 = bf16[8,24,1024]{2,1,0:T(8,128)(2,1)} fusion(bf16[8,24,1024]{2,1,0:T(8,128)(2,1)} %broadcast.60.clone.1, s32[128]{0:T(128)S(1)} %get-tuple-element.30, bf16[128,1024]{1,0:T(8,128)(2,1)S(1)} %reshape.137), kind=kCustom, calls=%fused_computation.3 | custom fusion | bytes 787456 | tf_op jit(solution)/shard_map/scatter | solution.py:78
  147.5 5.8 %all-to-all-start.2 = ((bf16[8,24,1024]{2,1,0:T(8,128)(2,1)}), bf16[8,24,1024]{2,1,0:T(8,128)(2,1)S(1)}, u32[]{:S(2)}, u32[]{:S(2)}) async-start(bf16[8,24,1024]{2,1,0:T(8,128)(2,1)} %scatter_fusion.1), calls=%async_computation.3 | async-start | bytes 786432 | tf_op jit(solution)/shard_map/all_to_all | solution.py:85
  153.2 0.0 reduce-scatter.5.cloned.1.call-start
  153.3 1.8 all-gather
  155.1 0.1 reshape.116
  155.2 2.4 all_gather.19
  157.5 0.6 fusion.3
  158.1 6.6 %all-to-all-done.2 = bf16[8,24,1024]{2,1,0:T(8,128)(2,1)S(1)} async-done(((bf16[8,24,1024]{2,1,0:T(8,128)(2,1)}), bf16[8,24,1024]{2,1,0:T(8,128)(2,1)S(1)}, u32[]{:S(2)}, u32[]{:S(2)}) %all-to-all-start.2) | async-done | bytes 393248 | tf_op jit(solution)/shard_map/all_to_all | solution.py:85
  164.7 2.4 all_gather.18
  167.1 2.7 multiply_reduce_fusion
  169.8 0.0 copy-start.6
  169.8 0.7 copy-done.6
  170.5 1.5 convolution_convert_fusion.2
  172.0 0.0 reduce-scatter.5.cloned.1.call-update
  172.0 0.0 reduce-scatter.3.cloned.1.call-start
  172.1 4.5 %fusion.8 = f32[512,4096]{1,0:T(8,128)} fusion(bf16[1,128,4096]{2,1,0:T(8,128)(2,1)S(1)} %copy-done.1, bf16[1,128,512]{2,1,0:T(8,128)(2,1)S(1)} %copy-done.8), kind=kOutput, calls=%fused_computation.20 | convolution fusion | flops 536870912 | bytes 9568256 | tf_op jit(solution)/shard_map/dot_general | solution.py:43
  176.6 0.0 reduce-scatter.3.cloned.1.call-update
  176.6 0.6 copy-done.12
  177.2 0.6 dynamic-slice
  178.5 0.1 convert_element_type.82
  178.6 2.5 all-reduce
  181.1 9.9 %all_to_all.55 = bf16[8,1,24]{2,1,0:T(2,128)(2,1)S(1)} all-to-all(bf16[8,1,24]{2,1,0:T(2,128)(2,1)S(1)} %copy.42), channel_id=1, replica_groups=mesh['groups'=2,'expert'=4,'dp'=2,'pair'=2] {'expert','dp'}, dimensions={0} | all-to-all | bytes 768 | tf_op jit(solution)/shard_map/all_to_all | solution.py:121
  190.9 3.6 %all-to-all-start.4 = ((bf16[8,24,1024]{2,1,0:T(8,128)(2,1)}), bf16[8,24,1024]{2,1,0:T(8,128)(2,1)S(1)}, u32[]{:S(2)}, u32[]{:S(2)}) async-start(bf16[8,24,1024]{2,1,0:T(8,128)(2,1)} %reduce-scatter.5.cloned.1.call-done), calls=%async_computation.6 | async-start | bytes 786432 | tf_op jit(solution)/shard_map/all_to_all | solution.py:120
  194.6 1.8 fusion
  196.4 1.9 fusion.1
  198.3 1.5 gather_fusion.1
  199.8 0.1 reshape.113
  199.9 0.7 copy.43
  200.6 4.6 %all-to-all-done.4 = bf16[8,24,1024]{2,1,0:T(8,128)(2,1)S(1)} async-done(((bf16[8,24,1024]{2,1,0:T(8,128)(2,1)}), bf16[8,24,1024]{2,1,0:T(8,128)(2,1)S(1)}, u32[]{:S(2)}, u32[]{:S(2)}) %all-to-all-start.4) | async-done | bytes 393248 | tf_op jit(solution)/shard_map/all_to_all | solution.py:120
  205.2 1.7 gather_fusion
  206.8 0.1 convert_element_type.77
  207.0 1.4 reduce
  208.4 78.1 %reduce-scatter.3.cloned.1.call-done = f32[512,2048]{1,0:T(8,128)} async-done(((f32[512,4096]{1,0:T(8,128)}), f32[512,2048]{1,0:T(8,128)}) %reduce-scatter.3.cloned.1.call-update) | async-done | bytes 4194320 | tf_op jit(solution)/shard_map/reduce_scatter | solution.py:47
  286.5 3.8 %convert_element_type.70 = bf16[512,2048]{1,0:T(8,128)(2,1)} convert(f32[512,2048]{1,0:T(8,128)} %reduce-scatter.3.cloned.1.call-done) | non-fusion elementwise | flops 1048576 | bytes 6291456 | tf_op jit(solution)/shard_map/convert_element_type | solution.py:47
  (32 shorter events, 0.1 us)
Async XLA Ops:
  7.2 150.4 %copy-start = (bf16[1,1024,512]{2,1,0:T(8,128)(2,1)S(1)}, bf16[1,1024,512]{2,1,0:T(8,128)(2,1)}, u32[]{:S(2)}) copy-start(bf16[1,1024,512]{2,1,0:T(8,128)(2,1)} %param.14) | copy-start | bytes 3145732
  7.2 1.5 copy-start.10
  7.2 1.9 copy-start.11
  7.2 27.4 %all-gather.4.cloned.1.call-start = ((), (), s32[]{:S(2)}) async-start(), calls=%async_computation.8 | async-start | bytes 1179648 | tf_op jit(solution)/shard_map/all_gather | solution.py:38
  7.9 84.5 %all-gather.6.cloned.1.call-start = ((), (), s32[]{:S(2)}) async-start(), calls=%async_computation.10 | async-start | bytes 6291456 | tf_op jit(solution)/shard_map/all_gather | solution.py:37
  17.0 80.2 %all-to-all-start = ((bf16[8,1,24]{2,1,0:T(2,128)(2,1)}), bf16[8,1,24]{2,1,0:T(2,128)(2,1)S(1)}, u32[]{:S(2)}, u32[]{:S(2)}) async-start(bf16[8,1,24]{2,1,0:T(2,128)(2,1)} %copy.39), calls=%async_computation.1 | async-start | bytes 8192 | tf_op jit(solution)/shard_map/all_to_all | solution.py:86
  24.2 77.6 %copy-start.9 = (bf16[1,16,4,1024]{3,2,1,0:T(4,128)(2,1)S(1)}, bf16[1,16,4,1024]{3,2,1,0:T(4,128)(2,1)}, u32[]{:S(2)}) copy-start(bf16[1,16,4,1024]{3,2,1,0:T(4,128)(2,1)} %param.10) | copy-start | bytes 393220
  97.2 24.8 %all-to-all-start.1 = ((bf16[8,16,512]{2,1,0:T(8,128)(2,1)}), bf16[8,16,512]{2,1,0:T(8,128)(2,1)S(1)}, u32[]{:S(2)}, u32[]{:S(2)}) async-start(bf16[8,16,512]{2,1,0:T(8,128)(2,1)} %bitcast.5), calls=%async_computation.2 | async-start | bytes 262144 | tf_op jit(solution)/shard_map/all_to_all | solution.py:50
  122.0 25.5 %all-to-all-start.3 = ((bf16[8,24,1024]{2,1,0:T(8,128)(2,1)}), bf16[8,24,1024]{2,1,0:T(8,128)(2,1)S(1)}, u32[]{:S(2)}, u32[]{:S(2)}) async-start(bf16[8,24,1024]{2,1,0:T(8,128)(2,1)} %scatter_fusion.2), calls=%async_computation.4 | async-start | bytes 786432 | tf_op jit(solution)/shard_map/all_to_all | solution.py:84
  147.5 17.2 %all-to-all-start.2 = ((bf16[8,24,1024]{2,1,0:T(8,128)(2,1)}), bf16[8,24,1024]{2,1,0:T(8,128)(2,1)S(1)}, u32[]{:S(2)}, u32[]{:S(2)}) async-start(bf16[8,24,1024]{2,1,0:T(8,128)(2,1)} %scatter_fusion.1), calls=%async_computation.3 | async-start | bytes 786432 | tf_op jit(solution)/shard_map/all_to_all | solution.py:85
  153.2 37.7 %reduce-scatter.5.cloned.1.call-start = ((), (), s32[]{:S(2)}) async-start(), calls=%async_computation.11 | async-start | bytes 1179648 | tf_op jit(solution)/shard_map/reduce_scatter | solution.py:104
  158.1 8.9 %copy-start.4 = (f32[384,512]{1,0:T(8,128)}, f32[384,512]{1,0:T(8,128)S(1)}, u32[]{:S(2)}) copy-start(f32[384,512]{1,0:T(8,128)S(1)} %fusion.3) | copy-start | bytes 2359300
  167.1 2.7 copy-start.2
  169.8 0.7 copy-start.6
  169.8 2.3 copy-start.1
  169.8 2.3 copy-start.8
  172.0 114.5 %reduce-scatter.3.cloned.1.call-start = ((), (), s32[]{:S(2)}) async-start(), calls=%async_computation.9 | async-start | bytes 12582912 | tf_op jit(solution)/shard_map/reduce_scatter | solution.py:47
  176.6 0.7 copy-start.12
  176.6 18.0 %copy-start.7 = (bf16[384,512]{1,0:T(8,128)(2,1)S(1)}, bf16[384,512]{1,0:T(8,128)(2,1)}, u32[]{:S(2)}) copy-start(bf16[384,512]{1,0:T(8,128)(2,1)} %copy-done.6) | copy-start | bytes 1179652
  176.6 19.8 %copy-start.3 = (bf16[16,24,1024]{2,1,0:T(8,128)(2,1)S(1)}, bf16[16,24,1024]{2,1,0:T(8,128)(2,1)}, u32[]{:S(2)}) copy-start(bf16[16,24,1024]{2,1,0:T(8,128)(2,1)} %copy-done.2) | copy-start | bytes 2359300
  190.9 14.2 %all-to-all-start.4 = ((bf16[8,24,1024]{2,1,0:T(8,128)(2,1)}), bf16[8,24,1024]{2,1,0:T(8,128)(2,1)S(1)}, u32[]{:S(2)}, u32[]{:S(2)}) async-start(bf16[8,24,1024]{2,1,0:T(8,128)(2,1)} %reduce-scatter.5.cloned.1.call-done), calls=%async_computation.6 | async-start | bytes 786432 | tf_op jit(solution)/shard_map/all_to_all | solution.py:120
  194.6 1.8 copy-start.5
Sparse Core Ops, SparseCore 0:
  9.6 24.9 all-gather.3
  36.1 56.2 all-gather.5
  172.1 7.3 reduce-scatter.4
  181.8 104.6 reduce-scatter.2
where the time goes:
time: 299 us; the launch traced here: 297 us
  waiting for transfers between devices  159 us (53%)
  local copies, waits for them, and re-layouts  54.7 us (18%)
  starting transfers between devices  26.4 us (9%)
  blocking collectives  18.9 us (6%)
  matrix products  17.6 us (6%)
  between operations  14.7 us (5%)
  other arithmetic  5.67 us (2%)
    reduce_scatter x1, waiting for transfers between devices, per_device(): lax.psum_scatter(partial_value, 'dp', scatter_dimension=1, tiled=True)  78.1 us
    all_gather x1, waiting for transfers between devices, per_device(): weight_rows = lax.all_gather(merge_weight, 'dp', axis=1, tiled=True)  57.9 us
    scatter x1, local copies, waits for them, and re-layouts, per_device(): send_heads = jnp.zeros((experts, capacity, head_dim), jnp.bfloat16).at[fl...  19.2 us
    scatter x1, local copies, waits for them, and re-layouts, per_device(): send_inputs = jnp.zeros((experts, capacity, head_dim), jnp.bfloat16).at[f...  19 us
    all_gather x1, waiting for transfers between devices, per_device(): lax.all_gather(out_grad, ('expert', 'pair'), axis=1, tiled=True)[0]  10.4 us
    all_to_all x1, blocking collectives, per_device(): lax.all_to_all(prob_low, ('expert', 'dp'), split_axis=0, concat_axis=0, t...  9.89 us
    all_to_all x1, starting transfers between devices, per_device(): lax.all_to_all(send_gates, ('expert', 'dp'), split_axis=0, concat_axis=0,...  7.25 us
    all_to_all x1, waiting for transfers between devices, per_device(): lax.all_to_all(send_heads, ('expert', 'dp'), split_axis=0, concat_axis=0,...  6.58 us
  transfers between devices with their start and end apart: 9, of which 5 were waited for; matrix products, arithmetic and copies ran while one was open for 23% of the time, Pallas kernels for 0%

commit v1 on v0

v1 whole, which is shorter than its diff:
```python
import jax
import jax.numpy as jnp
from jax import lax
from jax.sharding import PartitionSpec as P


def expert_block(inputs, head_part, gates, first, second):
    preact = jnp.dot(inputs, first, preferred_element_type=jnp.float32)
    activated, pullback = jax.vjp(jax.nn.gelu, preact)
    back_hidden = lax.dot_general(
        head_part, second, (((1,), (1,)), ((), ())), preferred_element_type=jnp.float32
    )
    prob_half = jnp.sum(activated * back_hidden, axis=1)
    scales = gates.astype(jnp.float32)[:, None]
    hidden_grad = pullback(scales * back_hidden)[0].astype(jnp.bfloat16)
    out_scaled = (scales * head_part.astype(jnp.float32)).astype(jnp.bfloat16)
    act_low = activated.astype(jnp.bfloat16)
    grad_first = lax.dot_general(
        inputs, hidden_grad, (((0,), (0,)), ((), ())), preferred_element_type=jnp.float32
    )
    grad_second = lax.dot_general(
        act_low, out_scaled, (((0,), (0,)), ((), ())), preferred_element_type=jnp.float32
    )
    input_half = lax.dot_general(
        hidden_grad, first, (((1,), (1,)), ((), ())), preferred_element_type=jnp.float32
    )
    return (input_half, prob_half, grad_first, grad_second)


def slots_of(routes, experts, capacity):
    flat = routes.reshape(-1)
    top = routes.shape[-1]
    onehot = (flat[:, None] == jnp.arange(experts, dtype=jnp.int32)[None, :]).astype(jnp.int32)
    rank = jnp.sum((jnp.cumsum(onehot, axis=0) - onehot) * onehot, axis=1)
    return (flat * capacity + rank).reshape(-1, top)


def per_device(
    out_grad, merged, sub_tokens, routes, gate_probs, merge_weight, expert_in, expert_out
):
    experts = lax.axis_size("expert") * lax.axis_size("dp")
    data_size = lax.axis_size("dp")
    length, feats = merged.shape[1:]
    positions, head_count, head_dim = sub_tokens.shape[1:]
    top_count = routes.shape[3]
    subs = positions * head_count
    routed_count = subs * top_count
    capacity = max(2, 3 * routed_count // (2 * experts))
    slot_count = experts * capacity
    columns = lax.all_to_all(out_grad[0], "dp", split_axis=1, concat_axis=0, tiled=True)
    width = columns.shape[1]
    tokens = lax.all_gather(columns, ("expert", "pair"), axis=0, tiled=False)
    tokens = tokens.reshape(-1, data_size, positions, width).transpose(1, 0, 2, 3)
    tokens = tokens.reshape(data_size * length, width)
    saved = lax.all_gather(merged[0], "dp", axis=0, tiled=True)
    partial = lax.dot_general(
        tokens, merge_weight, (((1,), (1,)), ((), ())), preferred_element_type=jnp.float32
    ).reshape(data_size, length, feats)
    partial = lax.all_to_all(partial, "dp", split_axis=0, concat_axis=0, tiled=True)
    head_block = jnp.sum(partial, axis=0).astype(jnp.bfloat16)
    head_grad = lax.all_to_all(
        head_block, ("expert", "pair"), split_axis=0, concat_axis=1, tiled=True
    ).reshape(subs, head_dim)
    merge_grad = lax.dot_general(
        saved, tokens, (((0,), (0,)), ((), ())), preferred_element_type=jnp.float32
    ).astype(jnp.bfloat16)

    slots = slots_of(routes[0], experts, capacity)
    numbers = jnp.arange(slot_count, dtype=jnp.int32)
    hits = (slots[None, :, :] == numbers[:, None, None]).astype(jnp.bfloat16)
    pick = jnp.sum(hits, axis=2)
    gates = jnp.sum(
        hits.astype(jnp.float32)
        * gate_probs[0].reshape(1, subs, top_count).astype(jnp.float32),
        axis=(1, 2),
    ).astype(jnp.bfloat16)
    extra = jnp.broadcast_to(gates[:, None], (slot_count, 128))

    def select(rows):
        return jnp.dot(pick, rows, preferred_element_type=jnp.float32).astype(jnp.bfloat16)

    send_inputs = jnp.concatenate(
        [select(sub_tokens[0].reshape(subs, head_dim)), extra], axis=1
    ).reshape(experts, capacity, head_dim + 128)
    send_heads = select(head_grad).reshape(experts, capacity, head_dim)

    def spread(rows):
        got = lax.all_to_all(rows, ("expert", "dp"), split_axis=0, concat_axis=0, tiled=True)
        return lax.all_gather(got, "pair", axis=0, tiled=True).reshape(-1, rows.shape[2])

    inputs = spread(send_inputs)
    heads = spread(send_heads)
    first = expert_in[0]
    second = expert_out[0]
    input_part, prob_part, grads_first, grads_second = expert_block(
        inputs[:, :head_dim], heads, inputs[:, head_dim], first, second
    )
    both = jnp.concatenate(
        [input_part, jnp.broadcast_to(prob_part[:, None], (prob_part.shape[0], 128))], axis=1
    ).astype(jnp.bfloat16)
    summed = lax.psum_scatter(
        both.reshape(2 * experts, capacity, head_dim + 128),
        "pair",
        scatter_dimension=0,
        tiled=True,
    )
    back = lax.all_to_all(summed, ("expert", "dp"), split_axis=0, concat_axis=0, tiled=True)
    back = back.reshape(slot_count, head_dim + 128)
    grad_sub = lax.dot_general(
        pick, back[:, :head_dim], (((0,), (0,)), ((), ())), preferred_element_type=jnp.float32
    ).astype(jnp.bfloat16)
    grad_probs = jnp.sum(
        hits.astype(jnp.float32) * back[:, head_dim].astype(jnp.float32)[:, None, None], axis=0
    ).astype(jnp.bfloat16)
    return (
        merge_grad,
        grad_sub.reshape(sub_tokens.shape),
        grad_probs.reshape(gate_probs.shape),
        grads_first.astype(jnp.bfloat16).reshape(expert_in.shape),
        grads_second.astype(jnp.bfloat16).reshape(expert_out.shape),
    )


def solution(mesh):
    placed = (
        P(("groups", "dp"), ("expert", "pair"), None),
        P(("groups", "dp"), None, ("expert", "pair")),
        P(("groups", "dp"), ("expert", "pair"), None, None),
        P(("groups", "dp"), ("expert", "pair"), None, None),
        P(("groups", "dp"), ("expert", "pair"), None, None),
        P(("expert", "pair"), "dp"),
        P(("expert", "dp"), None, "pair"),
        P(("expert", "dp"), "pair", None),
    )
    return jax.shard_map(
        per_device,
        mesh=mesh,
        in_specs=placed,
        out_specs=(
            P(("groups", "expert", "pair"), "dp"),
            P(("groups", "dp"), ("expert", "pair"), None, None),
            P(("groups", "dp"), ("expert", "pair"), None, None),
            P(("groups", "expert", "dp"), None, "pair"),
            P(("groups", "expert", "dp"), "pair", None),
        ),
        check_vma=False,
    )
```

time: 299 us -> 150 us (0.50)
  waiting for transfers between devices: 159 us -> 56.9 us
  local copies, waits for them, and re-layouts: 54.7 us -> 9.2 us
  starting transfers between devices: 26.4 us -> 21.7 us
  blocking collectives: 18.9 us -> 22.9 us
    reduce_scatter x2 -> x1, waiting for transfers between devices: 78.1 us -> 7.54 us  [per_device(): lax.psum_scatter(both.reshape(2 * experts, capacity, head_dim + 128), 'pa...]
    all_gather x2 -> x1, waiting for transfers between devices: 68.3 us -> 19.5 us  [per_device(): tokens = lax.all_gather(columns, ('expert', 'pair'), axis=0, tiled=False)]
    scatter x3 -> x0, local copies, waits for them, and re-layouts: 44.8 us -> none  [the longest x1 19.2 us: per_device(): send_heads = jnp.zeros((experts, capacity, head_dim), jnp.bfloat16).at[fl...]
    all_to_all x4, waiting for transfers between devices: 11.2 us -> 24 us  [the longest x2 17.9 us: spread(): lax.all_to_all(rows, ('expert', 'dp'), split_axis=0, concat_axis=0, tiled...]
    all_gather x3, blocking collectives: 6.51 us -> 14.3 us  [the longest x1 9.2 us: per_device(): saved = lax.all_gather(merged[0], 'dp', axis=0, tiled=True)]
    all_to_all x1, waiting for transfers between devices: 0.01 us -> 5.89 us  [per_device(): lax.all_to_all(head_block, ('expert', 'pair'), split_axis=0, concat_axis=...]
    all_to_all x4, starting transfers between devices: 21.6 us -> 17.7 us  [the longest x2 7.73 us: spread(): lax.all_to_all(rows, ('expert', 'dp'), split_axis=0, concat_axis=0, tiled...]
    gather x2 -> x0, local copies, waits for them, and re-layouts: 3.14 us -> none  [the longest x1 1.65 us: per_device(): back_inputs[flat_ids, slot_rank].astype(jnp.float32)]
  transfers between devices with their start and end apart: 9 -> 7, of which waited for: 5 -> 6; matrix products, arithmetic and copies ran while one was open for 23% -> 10% of each run, Pallas kernels for 0% -> 0%
where the time goes in v1:
time: 150 us; the launch traced here: 149 us
  waiting for transfers between devices  56.9 us (38%)
  blocking collectives  22.9 us (15%)
  starting transfers between devices  21.7 us (14%)
  matrix products  17.6 us (12%)
  between operations  14.2 us (9%)
  local copies, waits for them, and re-layouts  9.2 us (6%)
  other arithmetic  6.62 us (4%)
    all_gather x1, waiting for transfers between devices, per_device(): tokens = lax.all_gather(columns, ('expert', 'pair'), axis=0, tiled=False)  19.5 us
    all_to_all x2, waiting for transfers between devices, spread(): lax.all_to_all(rows, ('expert', 'dp'), split_axis=0, concat_axis=0, tiled...  17.9 us
    all_gather x1, blocking collectives, per_device(): saved = lax.all_gather(merged[0], 'dp', axis=0, tiled=True)  9.2 us
    all_to_all x1, blocking collectives, per_device(): lax.all_to_all(out_grad[0], 'dp', split_axis=1, concat_axis=0, tiled=True)  8.58 us
    all_to_all x2, starting transfers between devices, spread(): lax.all_to_all(rows, ('expert', 'dp'), split_axis=0, concat_axis=0, tiled...  7.73 us
    reduce_scatter x1, waiting for transfers between devices, per_device(): lax.psum_scatter(both.reshape(2 * experts, capacity, head_dim + 128), 'pa...  7.54 us
    all_to_all x1, waiting for transfers between devices, per_device(): lax.all_to_all(partial, 'dp', split_axis=0, concat_axis=0, tiled=True)  6.14 us
    all_to_all x1, waiting for transfers between devices, per_device(): lax.all_to_all(head_block, ('expert', 'pair'), split_axis=0, concat_axis=...  5.89 us
  transfers between devices with their start and end apart: 7, of which 6 were waited for; matrix products, arithmetic and copies ran while one was open for 10% of the time, Pallas kernels for 0%

profile of v1, /device:TPU:0, one launch (start us, length us, event | category | flops | bytes accessed | tf_op | source)
XLA Modules:
  0.0 149.2 jit_solution(10715208988955737119)
XLA Ops:
  7.2 0.0 copy-start
  7.2 0.0 all-gather.3.cloned.1.call-start
  7.2 1.1 all_to_all.34
  8.4 8.6 %all_to_all.49 = bf16[16,2,2048]{2,0,1:T(8,128)(2,1)} all-to-all(bf16[16,2,2048]{2,0,1:T(8,128)(2,1)S(1)} %copy.54), channel_id=1, replica_groups=mesh['groups'=2,'expert'=4,'dp'=2,'pair'=2] {'dp'}, dimensions={1} | all-to-all | bytes 262144 | tf_op jit(solution)/shard_map/all_to_all | solution.py:50
  17.0 0.0 all-gather.3.cloned.1.call-update
  17.0 0.8 copy.57
  17.8 0.7 broadcast_multiply_fusion
  18.5 0.1 copy.56
  18.6 0.1 mul.102
  18.7 0.8 copy.59
  19.5 0.1 reshape.122
  19.5 0.1 eq.28
  19.7 0.1 fusion.26
  19.8 0.2 reduce_window_sum.11
  20.0 0.2 select_reduce_fusion
  20.1 0.1 reduce_sum.60
  20.3 0.1 copy.58
  20.4 0.1 fusion.22
  20.5 19.5 %all-gather.3.cloned.1.call-done = bf16[8,32,2048]{2,1,0:T(8,128)(2,1)} async-done(((bf16[1,32,2048]{2,1,0:T(8,128)(2,1)}), bf16[8,32,2048]{2,1,0:T(8,128)(2,1)}) %all-gather.3.cloned.1.call-update) | async-done | bytes 1048592 | tf_op jit(solution)/shard_map/all_gather | solution.py:52
  40.0 1.3 copy.55
  41.3 0.0 copy-start.8
  41.3 1.5 %fusion = f32[2,128,512]{2,1,0:T(8,128)} fusion(bf16[2,128,2048]{2,1,0:T(8,128)(2,1)S(1)} %bitcast.58, bf16[512,2048]{1,0:T(8,128)(2,1)S(1)} %copy-done), kind=kOutput, calls=%fused_computation.1 | convolution fusion | flops 536870912 | bytes 3670016 | tf_op jit(solution)/shard_map/dot_general | solution.py:56
  42.8 4.2 %all-to-all-start.2 = ((f32[2,128,512]{2,1,0:T(8,128)}), f32[2,128,512]{2,1,0:T(8,128)}, u32[]{:S(2)}, u32[]{:S(2)}) async-start(f32[2,128,512]{2,1,0:T(8,128)} %fusion), calls=%async_computation.2 | async-start | bytes 1048576 | tf_op jit(solution)/shard_map/all_to_all | solution.py:59
  47.0 0.7 fusion.25
  47.7 0.7 reshape_squeeze.2
  48.4 1.2 convolution_convert_fusion.5
  49.6 6.1 %all-to-all-done.2 = f32[2,128,512]{2,1,0:T(8,128)} async-done(((f32[2,128,512]{2,1,0:T(8,128)}), f32[2,128,512]{2,1,0:T(8,128)}, u32[]{:S(2)}, u32[]{:S(2)}) %all-to-all-start.2) | async-done | bytes 524320 | tf_op jit(solution)/shard_map/all_to_all | solution.py:59
  55.8 1.8 %reduce_sum.63 = bf16[128,512]{1,0:T(8,128)(2,1)} reduce(f32[2,128,512]{2,1,0:T(8,128)} %all-to-all-done.2, f32[]{:T(128)} %constant.8.clone.1), dimensions={0}, to_apply=%region_4.5 | reduce | flops 65536 | bytes 655364 | tf_op jit(solution)/shard_map/reduce_sum | solution.py:60
  57.6 4.0 %all-to-all-start.3 = ((bf16[8,16,512]{2,1,0:T(8,128)(2,1)}), bf16[8,16,512]{2,1,0:T(8,128)(2,1)}, u32[]{:S(2)}, u32[]{:S(2)}) async-start(bf16[8,16,512]{2,1,0:T(8,128)(2,1)} %bitcast.68), calls=%async_computation.3 | async-start | bytes 262144 | tf_op jit(solution)/shard_map/all_to_all | solution.py:61
  61.6 0.1 broadcast_in_dim.6
  61.7 0.8 pad_maximum_fusion.1
  62.5 5.9 %all-to-all-done.3 = bf16[8,16,512]{2,1,0:T(8,128)(2,1)} async-done(((bf16[8,16,512]{2,1,0:T(8,128)(2,1)}), bf16[8,16,512]{2,1,0:T(8,128)(2,1)}, u32[]{:S(2)}, u32[]{:S(2)}) %all-to-all-start.3) | async-done | bytes 131104 | tf_op jit(solution)/shard_map/all_to_all | solution.py:61
  68.3 4.1 %all-to-all-start.1 = ((bf16[8,24,1152]{2,1,0:T(8,128)(2,1)}), bf16[8,24,1152]{2,1,0:T(8,128)(2,1)}, u32[]{:S(2)}, u32[]{:S(2)}) async-start(bf16[8,24,1152]{2,1,0:T(8,128)(2,1)} %bitcast.62), calls=%async_computation.1 | async-start | bytes 884736 | tf_op jit(solution)/shard_map/all_to_all | solution.py:88
  72.5 1.0 copy.61
  73.5 1.8 %convolution_convert_fusion.4 = bf16[192,1024]{1,0:T(8,128)(2,1)} fusion(bf16[192,64]{0,1:T(8,128)(2,1)} %fusion.25, bf16[64,1024]{1,0:T(8,128)(2,1)S(1)} %reshape.115), kind=kOutput, calls=%fused_computation.9 | convolution fusion | flops 25362432 | bytes 548864 | tf_op jit(solution)/shard_map/dot_general | solution.py:80
  75.3 9.9 %all-to-all-done.1 = bf16[8,24,1152]{2,1,0:T(8,128)(2,1)} async-done(((bf16[8,24,1152]{2,1,0:T(8,128)(2,1)}), bf16[8,24,1152]{2,1,0:T(8,128)(2,1)}, u32[]{:S(2)}, u32[]{:S(2)}) %all-to-all-start.1) | async-done | bytes 442400 | tf_op jit(solution)/shard_map/all_to_all | solution.py:88
  85.2 3.6 %all-to-all-start.4 = ((bf16[8,24,1024]{2,1,0:T(8,128)(2,1)}), bf16[8,24,1024]{2,1,0:T(8,128)(2,1)S(1)}, u32[]{:S(2)}, u32[]{:S(2)}) async-start(bf16[8,24,1024]{2,1,0:T(8,128)(2,1)} %bitcast.13), calls=%async_computation.4 | async-start | bytes 786432 | tf_op jit(solution)/shard_map/all_to_all | solution.py:88
  88.8 0.0 reduce-scatter.2.cloned.1.call-start
  88.8 2.7 %all_gather.18 = bf16[16,24,1152]{2,1,0:T(8,128)(2,1)S(1)} all-gather(bf16[8,24,1152]{2,1,0:T(8,128)(2,1)} %all-to-all-done.1), channel_id=1, replica_groups=mesh['groups'=2,'expert'=4,'dp'=2,'pair'=2] {'pair'}, dimensions={0}, use_global_device_ids=true | all-gather | bytes 1327104 | tf_op jit(solution)/shard_map/all_gather | solution.py:89
  91.5 0.9 copy-done.3
  92.4 0.1 convert_reduce_fusion
  92.5 8.0 %all-to-all-done.4 = bf16[8,24,1024]{2,1,0:T(8,128)(2,1)S(1)} async-done(((bf16[8,24,1024]{2,1,0:T(8,128)(2,1)}), bf16[8,24,1024]{2,1,0:T(8,128)(2,1)S(1)}, u32[]{:S(2)}, u32[]{:S(2)}) %all-to-all-start.4) | async-done | bytes 393248 | tf_op jit(solution)/shard_map/all_to_all | solution.py:88
  100.5 2.5 %all_gather.19 = bf16[16,24,1024]{2,1,0:T(8,128)(2,1)S(1)} all-gather(bf16[8,24,1024]{2,1,0:T(8,128)(2,1)S(1)} %all-to-all-done.4), channel_id=1, replica_groups=mesh['groups'=2,'expert'=4,'dp'=2,'pair'=2] {'pair'}, dimensions={0}, use_global_device_ids=true | all-gather | bytes 1179648 | tf_op jit(solution)/shard_map/all_gather | solution.py:89
  103.0 2.1 %fusion.7 = f32[384,512]{1,0:T(8,128)S(1)} fusion(bf16[384,1024]{1,0:T(8,128)(2,1)S(1)} %bitcast.60, bf16[1,512,1024]{2,1,0:T(8,128)(2,1)} %param.15), kind=kOutput, calls=%fused_computation.17 | convolution fusion | flops 402653184 | bytes 2621440 | tf_op jit(solution)/shard_map/dot_general | solution.py:10
  105.1 2.1 %fusion.15 = (bf16[384,512]{1,0:T(8,128)(2,1)}, bf16[384]{0:T(512)(128)(2,1)S(1)}, f32[384,512]{1,0:T(8,128)}) fusion(f32[384,512]{1,0:T(8,128)S(1)} %fusion.7, f32[384]{0:T(512)S(1)} %convert_reduce_fusion, bf16[1,1024,512]{2,1,0:T(8,128)(2,1)S(1)} %copy-done.9, bf16[384,1152]{1,0:T(8,128)(2,1)S(1)} %bitcast.64), kind=kOutput, calls=%fused_computation.26 | convolution fusion | flops 407371392 | bytes 3803904 | tf_op jit(solution)/shard_map/dot_general | solution.py:8
  107.3 0.1 reshape.124
  107.4 2.0 %convolution_convert_fusion.3 = bf16[16,24,1024]{2,1,0:T(8,128)(2,1)S(1)} fusion(bf16[16,24,512]{2,1,0:T(8,128)(2,1)} %bitcast.70, bf16[1,1024,512]{2,1,0:T(8,128)(2,1)} %param.14), kind=kOutput, calls=%fused_computation.6 | convolution fusion | flops 403046400 | bytes 2228224 | tf_op jit(solution)/shard_map/dot_general | solution.py:24
  109.3 0.0 copy-start.7
  109.3 0.1 broadcast_in_dim.8
  109.5 1.0 pad_maximum_fusion
  110.5 0.0 reduce-scatter.2.cloned.1.call-update
  110.5 7.5 %reduce-scatter.2.cloned.1.call-done = bf16[8,24,1152]{2,1,0:T(8,128)(2,1)} async-done(((bf16[16,24,1152]{2,1,0:T(8,128)(2,1)}), bf16[8,24,1152]{2,1,0:T(8,128)(2,1)}) %reduce-scatter.2.cloned.1.call-update) | async-done | bytes 442384 | tf_op jit(solution)/shard_map/reduce_scatter | solution.py:101
  118.0 5.7 %all-to-all-start.5 = ((bf16[8,24,1152]{2,1,0:T(8,128)(2,1)}), bf16[8,24,1152]{2,1,0:T(8,128)(2,1)}, u32[]{:S(2)}, u32[]{:S(2)}) async-start(bf16[8,24,1152]{2,1,0:T(8,128)(2,1)} %reduce-scatter.2.cloned.1.call-done), calls=%async_computation.6 | async-start | bytes 884736 | tf_op jit(solution)/shard_map/all_to_all | solution.py:107
  123.7 9.2 %all-gather = bf16[1,256,512]{2,1,0:T(8,128)(2,1)S(1)} all-gather(bf16[1,128,512]{2,1,0:T(8,128)(2,1)S(1)} %copy-done.7), channel_id=2, replica_groups=mesh['groups'=2,'expert'=4,'dp'=2,'pair'=2] {'dp'}, dimensions={1}, use_global_device_ids=true | all-gather | bytes 393216 | tf_op jit(solution)/shard_map/all_gather | solution.py:55
  133.0 2.1 %convolution_convert_fusion = bf16[512,2048]{1,0:T(8,128)(2,1)} fusion(bf16[256,2048]{1,0:T(8,128)(2,1)S(1)} %bitcast.59, bf16[1,256,512]{2,1,0:T(8,128)(2,1)S(1)} %all-gather), kind=kOutput, calls=%fused_computation | convolution fusion | flops 537919488 | bytes 3407872 | tf_op jit(solution)/shard_map/dot_general | solution.py:64
  135.0 1.7 %fusion.2 = bf16[1,1024,512]{2,1,0:T(8,128)(2,1)} fusion(bf16[384,512]{1,0:T(8,128)(2,1)S(1)} %copy-done.10, bf16[384,1152]{1,0:T(8,128)(2,1)S(1)} %bitcast.65), kind=kOutput, calls=%fused_computation.7 | convolution fusion | flops 403177472 | bytes 2228224 | tf_op jit(solution)/shard_map/dot_general | solution.py:18
  136.8 1.9 %fusion.3 = bf16[1,512,1024]{2,1,0:T(8,128)(2,1)} fusion(bf16[384,1024]{1,0:T(8,128)(2,1)S(1)} %bitcast.61, f32[384]{0:T(512)S(1)} %convert_reduce_fusion, f32[384,512]{1,0:T(8,128)S(1)} %copy-done.11), kind=kOutput, calls=%fused_computation.8 | convolution fusion | flops 406126592 | bytes 2622976 | tf_op jit(solution)/shard_map/dot_general | solution.py:21
  138.6 0.8 slice_convert_fusion
  139.5 1.2 convolution_convert_fusion.6
  140.6 0.1 copy.65
  140.7 0.2 fusion.23
  140.9 0.7 reshape.119
  141.6 0.1 convert_element_type.110
  141.7 0.7 copy.63
  (24 shorter events, 0.1 us)
Async XLA Ops:
  7.2 34.1 %copy-start = (bf16[512,2048]{1,0:T(8,128)(2,1)S(1)}, bf16[512,2048]{1,0:T(8,128)(2,1)}, u32[]{:S(2)}) copy-start(bf16[512,2048]{1,0:T(8,128)(2,1)} %param.13) | copy-start | bytes 6291460
  7.2 32.8 %all-gather.3.cloned.1.call-start = ((), (), s32[]{:S(2)}) async-start(), calls=%async_computation.7 | async-start | bytes 1179648 | tf_op jit(solution)/shard_map/all_gather | solution.py:52
  41.3 6.5 %copy-start.8 = (bf16[1,16,4,1024]{3,2,1,0:T(4,128)(2,1)S(1)}, bf16[1,16,4,1024]{3,2,1,0:T(4,128)(2,1)}, u32[]{:S(2)}) copy-start(bf16[1,16,4,1024]{3,2,1,0:T(4,128)(2,1)} %param.10) | copy-start | bytes 393220
  42.8 12.9 %all-to-all-start.2 = ((f32[2,128,512]{2,1,0:T(8,128)}), f32[2,128,512]{2,1,0:T(8,128)}, u32[]{:S(2)}, u32[]{:S(2)}) async-start(f32[2,128,512]{2,1,0:T(8,128)} %fusion), calls=%async_computation.2 | async-start | bytes 1048576 | tf_op jit(solution)/shard_map/all_to_all | solution.py:59
  57.6 10.8 %all-to-all-start.3 = ((bf16[8,16,512]{2,1,0:T(8,128)(2,1)}), bf16[8,16,512]{2,1,0:T(8,128)(2,1)}, u32[]{:S(2)}, u32[]{:S(2)}) async-start(bf16[8,16,512]{2,1,0:T(8,128)(2,1)} %bitcast.68), calls=%async_computation.3 | async-start | bytes 262144 | tf_op jit(solution)/shard_map/all_to_all | solution.py:61
  68.3 16.8 %all-to-all-start.1 = ((bf16[8,24,1152]{2,1,0:T(8,128)(2,1)}), bf16[8,24,1152]{2,1,0:T(8,128)(2,1)}, u32[]{:S(2)}, u32[]{:S(2)}) async-start(bf16[8,24,1152]{2,1,0:T(8,128)(2,1)} %bitcast.62), calls=%async_computation.1 | async-start | bytes 884736 | tf_op jit(solution)/shard_map/all_to_all | solution.py:88
  85.2 15.3 %all-to-all-start.4 = ((bf16[8,24,1024]{2,1,0:T(8,128)(2,1)}), bf16[8,24,1024]{2,1,0:T(8,128)(2,1)S(1)}, u32[]{:S(2)}, u32[]{:S(2)}) async-start(bf16[8,24,1024]{2,1,0:T(8,128)(2,1)} %bitcast.13), calls=%async_computation.4 | async-start | bytes 786432 | tf_op jit(solution)/shard_map/all_to_all | solution.py:88
  88.8 29.2 %reduce-scatter.2.cloned.1.call-start = ((), (), s32[]{:S(2)}) async-start(), calls=%async_computation.8 | async-start | bytes 1327104 | tf_op jit(solution)/shard_map/reduce_scatter | solution.py:101
  91.5 0.9 copy-start.3
  100.5 4.6 %copy-start.4 = (bf16[16,24,1152]{2,1,0:T(8,128)(2,1)S(1)}, bf16[16,24,1152]{2,1,0:T(8,128)(2,1)}, u32[]{:S(2)}) copy-start(bf16[16,24,1152]{2,1,0:T(8,128)(2,1)} %copy-done.3) | copy-start | bytes 2654212
  100.5 4.6 %copy-start.9 = (bf16[1,1024,512]{2,1,0:T(8,128)(2,1)S(1)}, bf16[1,1024,512]{2,1,0:T(8,128)(2,1)}, u32[]{:S(2)}) copy-start(bf16[1,1024,512]{2,1,0:T(8,128)(2,1)} %param.14) | copy-start | bytes 3145732
  103.0 4.3 %copy-start.1 = (bf16[16,24,1024]{2,1,0:T(8,128)(2,1)}, bf16[16,24,1024]{2,1,0:T(8,128)(2,1)S(1)}, u32[]{:S(2)}) copy-start(bf16[16,24,1024]{2,1,0:T(8,128)(2,1)S(1)} %all_gather.19) | copy-start | bytes 2359300
  109.3 14.4 %copy-start.7 = (bf16[1,128,512]{2,1,0:T(8,128)(2,1)S(1)}, bf16[1,128,512]{2,1,0:T(8,128)(2,1)}, u32[]{:S(2)}) copy-start(bf16[1,128,512]{2,1,0:T(8,128)(2,1)} %param.9) | copy-start | bytes 393220
  118.0 20.6 %all-to-all-start.5 = ((bf16[8,24,1152]{2,1,0:T(8,128)(2,1)}), bf16[8,24,1152]{2,1,0:T(8,128)(2,1)}, u32[]{:S(2)}, u32[]{:S(2)}) async-start(bf16[8,24,1152]{2,1,0:T(8,128)(2,1)} %reduce-scatter.2.cloned.1.call-done), calls=%async_computation.6 | async-start | bytes 884736 | tf_op jit(solution)/shard_map/all_to_all | solution.py:107
  132.9 2.1 %copy-start.5 = (bf16[16,24,1152]{2,1,0:T(8,128)(2,1)S(1)}, bf16[16,24,1152]{2,1,0:T(8,128)(2,1)}, u32[]{:S(2)}) copy-start(bf16[16,24,1152]{2,1,0:T(8,128)(2,1)} %copy-done.3) | copy-start | bytes 2654212
  132.9 2.1 %copy-start.10 = (bf16[384,512]{1,0:T(8,128)(2,1)S(1)}, bf16[384,512]{1,0:T(8,128)(2,1)}, u32[]{:S(2)}) copy-start(bf16[384,512]{1,0:T(8,128)(2,1)} %get-tuple-element.30) | copy-start | bytes 1179652
  135.0 1.7 %copy-start.2 = (bf16[16,24,1024]{2,1,0:T(8,128)(2,1)S(1)}, bf16[16,24,1024]{2,1,0:T(8,128)(2,1)}, u32[]{:S(2)}) copy-start(bf16[16,24,1024]{2,1,0:T(8,128)(2,1)} %copy-done.1) | copy-start | bytes 2359300
  135.0 1.7 %copy-start.11 = (f32[384,512]{1,0:T(8,128)S(1)}, f32[384,512]{1,0:T(8,128)}, u32[]{:S(2)}) copy-start(f32[384,512]{1,0:T(8,128)} %get-tuple-element.32) | copy-start | bytes 2359300
  136.7 2.7 %copy-start.6 = (bf16[192,64]{0,1:T(8,128)(2,1)S(1)}, bf16[192,64]{0,1:T(8,128)(2,1)}, u32[]{:S(2)}) copy-start(bf16[192,64]{0,1:T(8,128)(2,1)} %fusion.25) | copy-start | bytes 73732
Sparse Core Ops, SparseCore 0:
  17.1 22.7 all-gather.2
  110.6 7.3 reduce-scatter.1

commit v2 on v1

--- a/solution.py
+++ b/solution.py
@@ -1,6 +1,10 @@
+import functools
+
 import jax
 import jax.numpy as jnp
 from jax import lax
+from jax.experimental import pallas as pl
+from jax.experimental.pallas import tpu as pltpu
 from jax.sharding import PartitionSpec as P
 
 
@@ -35,7 +39,7 @@
     return (flat * capacity + rank).reshape(-1, top)
 
 
-def per_device(
+def spread_plan(
     out_grad, merged, sub_tokens, routes, gate_probs, merge_weight, expert_in, expert_out
 ):
     experts = lax.axis_size("expert") * lax.axis_size("dp")
@@ -121,6 +125,354 @@
     )
 
 
+MESH = pl.DeviceIdType.MESH
+LANES = 128
+
+
+def across(left, right, dims):
+    return lax.dot_general(left, right, ((dims[0], dims[1]), ((), ())), preferred_element_type=jnp.float32)
+
+
+def rows_of(value):
+    return value.astype(jnp.float32).reshape(-1, value.shape[-1]).astype(jnp.bfloat16)
+
+
+def layer_kernel(
+    e_size, d_size, capacity, heads,
+    ids_row, ids_col, gates_row, og, saved, subs, w_any, first_any, second_any,
+    merge_any, sub_out, probs_out, in_any, out_any,
+    w, first, second, merge_out, in_out, out_out,
+    og_buf, saved_buf, send_u, recv_u, send_g, recv_g, part_buf, home_buf, half_buf, pair_buf,
+    ret_buf, back_buf,
+    load_sem, store_sem, og_s, og_r, ogf_s, ogf_r, sv_s, sv_r, u_s, u_r, uf_s, uf_r, g_s, g_r, gf_s, gf_r,
+    pt_s, pt_r, hf_s, hf_r, rt_s, rt_r,
+):
+    e, d, p = lax.axis_index("expert"), lax.axis_index("dp"), lax.axis_index("pair")
+    owners = e_size * d_size
+    me = e * d_size + d
+    other = 1 - p
+    positions, wide = og.shape
+    half_cols = wide // d_size
+    feats = saved.shape[1]
+    head_dim = wide // heads
+    slot_count = owners * capacity
+    count = ids_row.shape[1]
+    sub_rows = count // 2
+
+    def place(t, q):
+        return {"expert": t // d_size, "dp": lax.rem(t, d_size), "pair": q}
+
+    def remote(src, dst, send, recv, t, q):
+        return pltpu.make_async_remote_copy(
+            src_ref=src, dst_ref=dst, send_sem=send, recv_sem=recv,
+            device_id=place(t, q), device_id_type=MESH,
+        )
+
+    loads = [
+        pltpu.make_async_copy(w_any, w, load_sem.at[0]),
+        pltpu.make_async_copy(first_any, first, load_sem.at[1]),
+        pltpu.make_async_copy(second_any, second, load_sem.at[2]),
+    ]
+    for load in loads:
+        load.start()
+
+    barrier = pltpu.get_barrier_semaphore()
+    mine = me * 2 + p
+    for step in range(1, 2 * owners):
+        q = lax.rem(mine + step, 2 * owners)
+        pl.semaphore_signal(
+            barrier, inc=1, device_id=place(q // 2, lax.rem(q, 2)), device_id_type=MESH
+        )
+
+    before = lax.broadcasted_iota(jnp.int32, (count, count), 0) < lax.broadcasted_iota(
+        jnp.int32, (count, count), 1
+    )
+    same = ids_col[...] == ids_row[...]
+    rank = jnp.sum(jnp.where(before & same, 1.0, 0.0), axis=0, keepdims=True).astype(jnp.int32)
+    slots = ids_row[...] * capacity + rank
+    hits = jnp.where(
+        lax.broadcasted_iota(jnp.int32, (slot_count, count), 0) == slots, 1.0, 0.0
+    )
+    pick = (hits[:, :sub_rows] + hits[:, sub_rows:]).astype(jnp.bfloat16)
+    gate = jnp.sum(hits * gates_row[...], axis=1, keepdims=True)
+    stacked = jnp.concatenate(
+        [subs[:, h * head_dim : (h + 1) * head_dim] for h in range(heads)], axis=0
+    )
+    send_u[:, :, :head_dim] = (
+        across(pick, stacked, ((1,), (0,))).reshape(owners, capacity, head_dim).astype(jnp.bfloat16)
+    )
+    send_u[:, :, head_dim:] = (
+        jnp.broadcast_to(gate, (slot_count, LANES))
+        .reshape(owners, capacity, LANES)
+        .astype(jnp.bfloat16)
+    )
+    pl.semaphore_wait(barrier, 2 * owners - 1)
+
+    sends = []
+
+    def go(copy):
+        copy.start()
+        sends.append(copy)
+
+    def columns(t):
+        return og.at[:, pl.ds(pl.multiple_of(lax.rem(t, d_size) * half_cols, LANES), half_cols)]
+
+    for step in range(1, owners):
+        t = lax.rem(me + step, owners)
+        go(remote(columns(t), og_buf.at[p, me], og_s.at[step], og_r.at[me], t, p))
+    go(remote(columns(me), og_buf.at[p, me], ogf_s.at[me], ogf_r.at[me], me, other))
+    own_og = pltpu.make_async_copy(columns(me), og_buf.at[p, me], load_sem.at[3])
+    own_og.start()
+    for step in range(1, d_size):
+        t = e * d_size + lax.rem(d + step, d_size)
+        go(remote(saved, saved_buf.at[d], sv_s.at[step], sv_r.at[d], t, p))
+    saved_buf[d] = saved[...]
+    for step in range(1, owners):
+        t = lax.rem(me + step, owners)
+        go(remote(send_u.at[t], recv_u.at[p, me], u_s.at[step], u_r.at[me], t, p))
+    go(remote(send_u.at[me], recv_u.at[p, me], uf_s.at[me], uf_r.at[me], me, other))
+    recv_u[p, me] = send_u[me]
+
+    def pass_on(buf, recv, fsend, frecv):
+        for step in range(1, owners):
+            t = lax.rem(me + owners - step, owners)
+            remote(buf.at[p, t], buf.at[p, t], fsend.at[t], recv.at[t], me, other).wait_recv()
+            go(remote(buf.at[p, t], buf.at[p, t], fsend.at[t], frecv.at[t], me, other))
+
+    def from_pair(buf, fsend, frecv):
+        for t in range(owners):
+            remote(
+                buf.at[other, t], buf.at[other, t], fsend.at[t], frecv.at[t], me, other
+            ).wait_recv()
+
+    pass_on(og_buf, og_r, ogf_s, ogf_r)
+    own_og.wait()
+    loads[0].wait()
+    from_pair(og_buf, ogf_s, ogf_r)
+    tokens = og_buf[...].reshape(2 * owners * positions, half_cols)
+    part_buf[...] = (
+        across(tokens, w[...], ((1,), (1,)))
+        .astype(jnp.bfloat16)
+        .reshape(2, owners, positions, feats)
+    )
+    for step in range(1, 2 * owners):
+        q = lax.rem(mine + step, 2 * owners)
+        t, qp = q // 2, lax.rem(q, 2)
+        go(remote(part_buf.at[qp, t], home_buf.at[p, me], pt_s.at[step], pt_r.at[p, me], t, qp))
+    home_buf[p, me] = part_buf[p, me]
+    for step in range(1, 2 * owners):
+        q = lax.rem(mine + 2 * owners - step, 2 * owners)
+        t, qp = q // 2, lax.rem(q, 2)
+        remote(
+            home_buf.at[qp, t], home_buf.at[qp, t], pt_s.at[step], pt_r.at[qp, t], me, other
+        ).wait_recv()
+    blocks = []
+    for i in range(e_size):
+        for q in range(2):
+            total = home_buf[q, i * d_size].astype(jnp.float32)
+            for j in range(1, d_size):
+                total = total + home_buf[q, i * d_size + j].astype(jnp.float32)
+            blocks.append(total.astype(jnp.bfloat16))
+    per_head = head_dim // feats
+    head_rows = jnp.concatenate(
+        [
+            jnp.concatenate(blocks[h * per_head : (h + 1) * per_head], axis=1)
+            for h in range(heads)
+        ],
+        axis=0,
+    )
+    send_g[...] = (
+        across(pick, head_rows, ((1,), (0,)))
+        .reshape(owners, capacity, head_dim)
+        .astype(jnp.bfloat16)
+    )
+    for step in range(1, owners):
+        t = lax.rem(me + step, owners)
+        go(remote(send_g.at[t], recv_g.at[p, me], g_s.at[step], g_r.at[me], t, p))
+    go(remote(send_g.at[me], recv_g.at[p, me], gf_s.at[me], gf_r.at[me], me, other))
+    recv_g[p, me] = send_g[me]
+
+    pass_on(recv_u, u_r, uf_s, uf_r)
+    for step in range(1, d_size):
+        j = lax.rem(d + step, d_size)
+        remote(saved, saved_buf.at[j], sv_s.at[step], sv_r.at[j], me, other).wait_recv()
+    ordered = jnp.concatenate(
+        [
+            saved_buf[j, (i * 2 + q) * positions : (i * 2 + q + 1) * positions, :]
+            for q in range(2)
+            for i in range(e_size)
+            for j in range(d_size)
+        ],
+        axis=0,
+    )
+    merge_out[...] = across(ordered, tokens, ((0,), (0,))).astype(jnp.bfloat16)
+    stores = [pltpu.make_async_copy(merge_out, merge_any, store_sem.at[0])]
+    stores[0].start()
+    from_pair(recv_u, uf_s, uf_r)
+    inputs = rows_of(recv_u[:, :, :, :head_dim])
+    scales = recv_u[:, :, :, head_dim:].astype(jnp.float32).reshape(-1, LANES)[:, :1]
+    loads[1].wait()
+    loads[2].wait()
+    preact = across(inputs, first[...], ((1,), (0,)))
+    root = 0.7978845608028654
+    bend = jnp.tanh(root * (preact + 0.044715 * (preact * preact * preact)))
+    activated = 0.5 * preact * (1.0 + bend)
+    slope = 0.5 * (1.0 + bend) + 0.5 * preact * (1.0 - bend * bend) * (
+        root * (1.0 + 3.0 * 0.044715 * (preact * preact))
+    )
+
+    pass_on(recv_g, g_r, gf_s, gf_r)
+    from_pair(recv_g, gf_s, gf_r)
+    grads = rows_of(recv_g[...])
+    back = across(grads, second[...], ((1,), (1,)))
+    hidden = (slope * (scales * back)).astype(jnp.bfloat16)
+    half_buf[:, :, :, head_dim:] = (
+        jnp.broadcast_to(
+            jnp.sum(activated * back, axis=1, keepdims=True), (2 * slot_count, LANES)
+        )
+        .reshape(2, owners, capacity, LANES)
+        .astype(jnp.bfloat16)
+    )
+    half_buf[:, :, :, :head_dim] = (
+        across(hidden, first[...], ((1,), (1,)))
+        .reshape(2, owners, capacity, head_dim)
+        .astype(jnp.bfloat16)
+    )
+    order = [lax.rem(me + step, owners) for step in list(range(1, owners)) + [0]]
+    for t in order:
+        go(remote(half_buf.at[other, t], pair_buf.at[t], hf_s.at[t], hf_r.at[t], me, other))
+    for step, t in enumerate(order):
+        remote(half_buf.at[other, t], pair_buf.at[t], hf_s.at[t], hf_r.at[t], me, other).wait_recv()
+        ret_buf[t] = (
+            half_buf[p, t].astype(jnp.float32) + pair_buf[t].astype(jnp.float32)
+        ).astype(jnp.bfloat16)
+        if step < owners - 1:
+            go(remote(ret_buf.at[t], back_buf.at[me], rt_s.at[step], rt_r.at[me], t, p))
+    back_buf[me] = ret_buf[me]
+
+    in_out[...] = across(inputs, hidden, ((0,), (0,))).astype(jnp.bfloat16)
+    stores.append(pltpu.make_async_copy(in_out, in_any, store_sem.at[1]))
+    stores[1].start()
+    scaled = (scales * grads.astype(jnp.float32)).astype(jnp.bfloat16)
+    out_out[...] = across(activated.astype(jnp.bfloat16), scaled, ((0,), (0,))).astype(jnp.bfloat16)
+    stores.append(pltpu.make_async_copy(out_out, out_any, store_sem.at[2]))
+    stores[2].start()
+
+    for step in range(1, owners):
+        t = lax.rem(me + owners - step, owners)
+        remote(ret_buf.at[t], back_buf.at[t], rt_s.at[step], rt_r.at[t], me, other).wait_recv()
+    returned = rows_of(back_buf[...])
+    gathered = across(pick, returned[:, :head_dim], ((0,), (0,)))
+    for h in range(heads):
+        sub_out[:, h * head_dim : (h + 1) * head_dim] = gathered[
+            h * positions : (h + 1) * positions
+        ].astype(jnp.bfloat16)
+    probs_out[...] = across(
+        hits.astype(jnp.bfloat16), returned[:, head_dim:], ((0,), (0,))
+    ).astype(jnp.bfloat16)
+    for copy in sends:
+        copy.wait_send()
+    for store in stores:
+        store.wait()
+
+
+def fused(out_grad, merged, sub_tokens, routes, gate_probs, merge_weight, expert_in, expert_out):
+    e_size, d_size = lax.axis_size("expert"), lax.axis_size("dp")
+    owners = e_size * d_size
+    length, feats = merged.shape[1:]
+    positions, heads, head_dim = sub_tokens.shape[1:]
+    top = routes.shape[3]
+    count = positions * heads * top
+    capacity = max(2, 3 * count // (2 * owners))
+    wide = out_grad.shape[2]
+    half_cols = wide // d_size
+    half_units = expert_in.shape[2]
+    padded = head_dim + LANES
+    ids = routes[0].transpose(2, 1, 0).reshape(count)
+    gates = gate_probs[0].transpose(2, 1, 0).reshape(1, count).astype(jnp.float32)
+    low = jnp.bfloat16
+    dma = pltpu.SemaphoreType.DMA
+    vmem = pl.BlockSpec(memory_space=pltpu.VMEM)
+    anywhere = pl.BlockSpec(memory_space=pl.ANY)
+    one, two = dma((owners,)), dma((2 * owners,))
+    merge_grad, grad_sub, probs, grad_in, grad_out = pl.pallas_call(
+        functools.partial(layer_kernel, e_size, d_size, capacity, heads),
+        out_shape=(
+            jax.ShapeDtypeStruct(merge_weight.shape, low),
+            jax.ShapeDtypeStruct((positions, wide), low),
+            jax.ShapeDtypeStruct((count, LANES), low),
+            jax.ShapeDtypeStruct((head_dim, half_units), low),
+            jax.ShapeDtypeStruct((half_units, head_dim), low),
+        ),
+        in_specs=[vmem] * 6 + [anywhere] * 3,
+        out_specs=(anywhere, vmem, vmem, anywhere, anywhere),
+        scratch_shapes=[
+            pltpu.VMEM(merge_weight.shape, low),
+            pltpu.VMEM((head_dim, half_units), low),
+            pltpu.VMEM((half_units, head_dim), low),
+            pltpu.VMEM(merge_weight.shape, low),
+            pltpu.VMEM((head_dim, half_units), low),
+            pltpu.VMEM((half_units, head_dim), low),
+            pltpu.VMEM((2, owners, positions, half_cols), low),
+            pltpu.VMEM((d_size, length, feats), low),
+            pltpu.VMEM((owners, capacity, padded), low),
+            pltpu.VMEM((2, owners, capacity, padded), low),
+            pltpu.VMEM((owners, capacity, head_dim), low),
+            pltpu.VMEM((2, owners, capacity, head_dim), low),
+            pltpu.VMEM((2, owners, positions, feats), low),
+            pltpu.VMEM((2, owners, positions, feats), low),
+            pltpu.VMEM((2, owners, capacity, padded), low),
+            pltpu.VMEM((owners, capacity, padded), low),
+            pltpu.VMEM((owners, capacity, padded), low),
+            pltpu.VMEM((owners, capacity, padded), low),
+            dma((4,)), dma((3,)),
+            one, one, one, one,
+            dma((d_size,)), dma((d_size,)),
+            one, one, one, one,
+            one, one, one, one,
+            two, dma((2, owners)),
+            one, one, one, one,
+        ],
+        compiler_params=pltpu.CompilerParams(
+            collective_id=0, has_side_effects=True, vmem_limit_bytes=48 * 1024 * 1024
+        ),
+    )(
+        ids.reshape(1, count), ids.reshape(count, 1), gates,
+        out_grad[0], merged[0], sub_tokens[0].reshape(positions, wide),
+        merge_weight, expert_in[0], expert_out[0],
+    )
+    grad_probs = probs[:, 0].reshape(top, heads, positions).transpose(2, 1, 0)
+    return (
+        merge_grad,
+        grad_sub.reshape(sub_tokens.shape),
+        grad_probs.reshape(gate_probs.shape),
+        grad_in[None],
+        grad_out[None],
+    )
+
+
+def fits(out_grad, merged, sub_tokens, routes, gate_probs, merge_weight, expert_in, expert_out):
+    owners = lax.axis_size("expert") * lax.axis_size("dp")
+    positions, heads, head_dim = sub_tokens.shape[1:]
+    count = positions * heads * routes.shape[3]
+    capacity = max(2, 3 * count // (2 * owners))
+    return (
+        lax.axis_size("pair") == 2
+        and routes.shape[3] == 2
+        and capacity % 8 == 0
+        and positions % 16 == 0
+        and head_dim % merged.shape[2] == 0
+        and owners * positions <= 128
+        and expert_in.shape[0] == 1
+    )
+
+
+def per_device(*arrays):
+    if fits(*arrays):
+        return fused(*arrays)
+    return spread_plan(*arrays)
+
+
 def solution(mesh):
     placed = (
         P(("groups", "dp"), ("expert", "pair"), None),

time: 150 us -> 71.9 us (0.48)
  waiting for transfers between devices: 56.9 us -> 0 us
  Pallas kernels: 0 us -> 56.7 us
  blocking collectives: 22.9 us -> 0 us
  starting transfers between devices: 21.7 us -> 0 us
  matrix products: 17.6 us -> 0 us
  between operations: 14.2 us -> 0.67 us
  other arithmetic: 6.62 us -> 0 us
  local copies, waits for them, and re-layouts: 9.2 us -> 13.5 us
    pallas_call x0 -> x1, Pallas kernels: none -> 56.7 us  [fused(): pl.pallas_call(functools.partial(layer_kernel, e_size, d_size, capacity,...]
    all_to_all x5 -> x0, waiting for transfers between devices: 29.9 us -> none  [the longest x2 17.9 us: spread(): lax.all_to_all(rows, ('expert', 'dp'), split_axis=0, concat_axis=0, tiled...]
    all_to_all x5 -> x0, starting transfers between devices: 21.7 us -> none  [the longest x2 7.73 us: spread(): lax.all_to_all(rows, ('expert', 'dp'), split_axis=0, concat_axis=0, tiled...]
    all_gather x1 -> x0, waiting for transfers between devices: 19.5 us -> none  [per_device(): tokens = lax.all_gather(columns, ('expert', 'pair'), axis=0, tiled=False)]
    dot_general x10 -> x0, matrix products: 17.6 us -> none  [the longest x2 2.99 us: select(): jnp.dot(pick, rows, preferred_element_type=jnp.float32).astype(jnp.bfloat16)]
    all_gather x3 -> x0, blocking collectives: 14.3 us -> none  [the longest x1 9.2 us: per_device(): saved = lax.all_gather(merged[0], 'dp', axis=0, tiled=True)]
    unnamed x27 -> x14, local copies, waits for them, and re-layouts: 2.51 us -> 11.6 us
    all_to_all x1 -> x0, blocking collectives: 8.58 us -> none  [per_device(): lax.all_to_all(out_grad[0], 'dp', split_axis=1, concat_axis=0, tiled=True)]
  transfers between devices with their start and end apart: 7 -> 0, of which waited for: 6 -> 0; matrix products, arithmetic and copies ran while one was open for 10% -> 0% of each run, Pallas kernels for 0% -> 0%
where the time goes in v2:
time: 71.9 us; the launch traced here: 70.8 us
  Pallas kernels  56.7 us (79%)
  local copies, waits for them, and re-layouts  13.5 us (19%)
    pallas_call x1, Pallas kernels, fused(): pl.pallas_call(functools.partial(layer_kernel, e_size, d_size, capacity,...  56.7 us
    unnamed x14, local copies, waits for them, and re-layouts  11.6 us

profile of v2, /device:TPU:0, one launch (start us, length us, event | category | flops | bytes accessed | tf_op | source)
XLA Modules:
  0.0 70.8 jit_solution(12113871303472531244)
XLA Ops:
  0.6 0.7 copy.25
  1.3 0.1 reshape_reshape.6.ids_row
  1.4 0.7 copy.24
  2.1 0.1 reshape.35.gates_row
  2.2 0.1 reshape_reshape.8.ids_col
  2.3 0.9 %copy.21 = bf16[2,8,4,1024]{3,1,2,0:T(8,128)(2,1)S(1)} copy(bf16[2,8,4,1024]{3,2,1,0:T(4,128)(2,1)} %bitcast.29) | data formatting | bytes 262144
  3.2 0.0 copy-start
  3.2 1.2 %copy-done = bf16[1,1024,512]{2,1,0:T(8,128)(2,1)S(1)} copy-done((bf16[1,1024,512]{2,1,0:T(8,128)(2,1)S(1)}, bf16[1,1024,512]{2,1,0:T(8,128)(2,1)}, u32[]{:S(2)}) %copy-start) | copy-done | bytes 1048600
  4.5 0.0 copy-start.1
  4.5 1.2 %copy-done.1 = bf16[1,512,1024]{2,1,0:T(8,128)(2,1)S(1)} copy-done((bf16[1,512,1024]{2,1,0:T(8,128)(2,1)S(1)}, bf16[1,512,1024]{2,1,0:T(8,128)(2,1)}, u32[]{:S(2)}) %copy-start.1) | copy-done | bytes 1048600
  5.7 0.0 copy-start.2
  5.7 0.9 %copy-done.2 = bf16[1,16,4096]{2,1,0:T(8,128)(2,1)S(1)} copy-done((bf16[1,16,4096]{2,1,0:T(8,128)(2,1)S(1)}, bf16[1,16,4096]{2,1,0:T(8,128)(2,1)}, u32[]{:S(2)}) %copy-start.2) | copy-done | bytes 131096
  6.6 0.0 copy-start.3
  6.6 0.9 %copy-done.3 = bf16[1,128,512]{2,1,0:T(8,128)(2,1)S(1)} copy-done((bf16[1,128,512]{2,1,0:T(8,128)(2,1)S(1)}, bf16[1,128,512]{2,1,0:T(8,128)(2,1)}, u32[]{:S(2)}) %copy-start.3) | copy-done | bytes 131096
  7.5 56.7 %shard_map.119 = (bf16[512,2048]{1,0:T(8,128)(2,1)}, bf16[16,4096]{1,0:T(8,128)(2,1)S(1)}, bf16[128,128]{1,0:T(8,128)(2,1)S(1)}, bf16[1024,512]{1,0:T(8,128)(2,1)S(1)}, bf16[512,1024]{1,0:T(8,128)(2,1)S(1)}) custom-call(s32[1,128]{1,0:T(1,128)S(1)} %reshape_reshape.6.ids_row, s32[128,1]{1,0:T(8,128)S(1)} %reshape_reshape.8.ids_col, ...), custom_call_target="tpu_custom_call" | custom-call | tf_op jit(solution)/shard_map/pallas_call | solution.py:398
  64.2 0.1 slice_reduce_fusion
  64.3 0.1 reshape_squeeze.7
  64.4 0.6 copy.20
  65.0 0.7 %reshape.33 = bf16[1,16,4,1024]{3,2,1,0:T(4,128)(2,1)} reshape(bf16[16,4096]{1,0:T(8,128)(2,1)S(1)} %get-tuple-element.11) | data formatting | bytes 262144 | tf_op jit(solution)/shard_map/reshape | solution.py:447
  65.7 3.2 %copy.29 = bf16[512,2048]{1,0:T(8,128)(2,1)} copy(bf16[512,2048]{1,0:T(8,128)(2,1)} %get-tuple-element.30) | data formatting | bytes 4194304
  68.9 1.0 %copy.30 = bf16[1,1024,512]{2,1,0:T(8,128)(2,1)} copy(bf16[1,1024,512]{2,1,0:T(8,128)(2,1)S(1)} %bitcast.25) | data formatting | bytes 2097152
  69.9 1.0 %copy.31 = bf16[1,512,1024]{2,1,0:T(8,128)(2,1)} copy(bf16[1,512,1024]{2,1,0:T(8,128)(2,1)S(1)} %bitcast.24) | data formatting | bytes 2097152
Async XLA Ops:
  3.2 1.2 %copy-start = (bf16[1,1024,512]{2,1,0:T(8,128)(2,1)S(1)}, bf16[1,1024,512]{2,1,0:T(8,128)(2,1)}, u32[]{:S(2)}) copy-start(bf16[1,1024,512]{2,1,0:T(8,128)(2,1)} %param.14) | copy-start | bytes 3145732
  4.5 1.2 %copy-start.1 = (bf16[1,512,1024]{2,1,0:T(8,128)(2,1)S(1)}, bf16[1,512,1024]{2,1,0:T(8,128)(2,1)}, u32[]{:S(2)}) copy-start(bf16[1,512,1024]{2,1,0:T(8,128)(2,1)} %param.15) | copy-start | bytes 3145732
  5.7 0.9 %copy-start.2 = (bf16[1,16,4096]{2,1,0:T(8,128)(2,1)S(1)}, bf16[1,16,4096]{2,1,0:T(8,128)(2,1)}, u32[]{:S(2)}) copy-start(bf16[1,16,4096]{2,1,0:T(8,128)(2,1)} %param.8) | copy-start | bytes 393220
  6.6 0.9 %copy-start.3 = (bf16[1,128,512]{2,1,0:T(8,128)(2,1)S(1)}, bf16[1,128,512]{2,1,0:T(8,128)(2,1)}, u32[]{:S(2)}) copy-start(bf16[1,128,512]{2,1,0:T(8,128)(2,1)} %param.9) | copy-start | bytes 393220

commit v3 on v2

--- a/solution.py
+++ b/solution.py
@@ -139,9 +139,9 @@
 
 def layer_kernel(
     e_size, d_size, capacity, heads,
-    ids_row, ids_col, gates_row, og, saved, subs, w_any, first_any, second_any,
-    merge_any, sub_out, probs_out, in_any, out_any,
-    w, first, second, merge_out, in_out, out_out,
+    ids_any, gates_any, og_any, saved_any, subs, w_any, first_any, second_any,
+    tokens_any, ordered_out, sub_out, probs_out, in_any, out_any,
+    ids_in, gates_in, og, saved, w, first, second, in_out, out_out,
     og_buf, saved_buf, send_u, recv_u, send_g, recv_g, part_buf, home_buf, half_buf, pair_buf,
     ret_buf, back_buf,
     load_sem, store_sem, og_s, og_r, ogf_s, ogf_r, sv_s, sv_r, u_s, u_r, uf_s, uf_r, g_s, g_r, gf_s, gf_r,
@@ -156,8 +156,13 @@
     feats = saved.shape[1]
     head_dim = wide // heads
     slot_count = owners * capacity
-    count = ids_row.shape[1]
+    count = positions * heads * 2
     sub_rows = count // 2
+
+    def in_row(ref):
+        pieces = [ref[h, k : k + 1, :].astype(jnp.float32) for k in range(2) for h in range(heads)]
+        return jnp.concatenate(pieces, axis=1)
+
 
     def place(t, q):
         return {"expert": t // d_size, "dp": lax.rem(t, d_size), "pair": q}
@@ -168,12 +173,18 @@
             device_id=place(t, q), device_id_type=MESH,
         )
 
+    here = [
+        pltpu.make_async_copy(og_any, og, load_sem.at[4]),
+        pltpu.make_async_copy(saved_any, saved, load_sem.at[5]),
+        pltpu.make_async_copy(ids_any, ids_in, load_sem.at[6]),
+        pltpu.make_async_copy(gates_any, gates_in, load_sem.at[7]),
+    ]
     loads = [
         pltpu.make_async_copy(w_any, w, load_sem.at[0]),
         pltpu.make_async_copy(first_any, first, load_sem.at[1]),
         pltpu.make_async_copy(second_any, second, load_sem.at[2]),
     ]
-    for load in loads:
+    for load in here + loads:
         load.start()
 
     barrier = pltpu.get_barrier_semaphore()
@@ -184,28 +195,8 @@
             barrier, inc=1, device_id=place(q // 2, lax.rem(q, 2)), device_id_type=MESH
         )
 
-    before = lax.broadcasted_iota(jnp.int32, (count, count), 0) < lax.broadcasted_iota(
-        jnp.int32, (count, count), 1
-    )
-    same = ids_col[...] == ids_row[...]
-    rank = jnp.sum(jnp.where(before & same, 1.0, 0.0), axis=0, keepdims=True).astype(jnp.int32)
-    slots = ids_row[...] * capacity + rank
-    hits = jnp.where(
-        lax.broadcasted_iota(jnp.int32, (slot_count, count), 0) == slots, 1.0, 0.0
-    )
-    pick = (hits[:, :sub_rows] + hits[:, sub_rows:]).astype(jnp.bfloat16)
-    gate = jnp.sum(hits * gates_row[...], axis=1, keepdims=True)
-    stacked = jnp.concatenate(
-        [subs[:, h * head_dim : (h + 1) * head_dim] for h in range(heads)], axis=0
-    )
-    send_u[:, :, :head_dim] = (
-        across(pick, stacked, ((1,), (0,))).reshape(owners, capacity, head_dim).astype(jnp.bfloat16)
-    )
-    send_u[:, :, head_dim:] = (
-        jnp.broadcast_to(gate, (slot_count, LANES))
-        .reshape(owners, capacity, LANES)
-        .astype(jnp.bfloat16)
-    )
+    for load in here:
+        load.wait()
     pl.semaphore_wait(barrier, 2 * owners - 1)
 
     sends = []
@@ -227,6 +218,30 @@
         t = e * d_size + lax.rem(d + step, d_size)
         go(remote(saved, saved_buf.at[d], sv_s.at[step], sv_r.at[d], t, p))
     saved_buf[d] = saved[...]
+    rows_at = lax.broadcasted_iota(jnp.int32, (count, count), 0)
+    lanes_at = lax.broadcasted_iota(jnp.int32, (count, count), 1)
+    ids_row, gates_row = in_row(ids_in), in_row(gates_in)
+    ids_col = jnp.sum(jnp.where(rows_at == lanes_at, ids_row, 0.0), axis=1, keepdims=True)
+    rank = jnp.sum(
+        jnp.where((rows_at < lanes_at) & (ids_col == ids_row), 1.0, 0.0), axis=0, keepdims=True
+    )
+    slots = (ids_row * capacity + rank).astype(jnp.int32)
+    hits = jnp.where(
+        lax.broadcasted_iota(jnp.int32, (slot_count, count), 0) == slots, 1.0, 0.0
+    )
+    pick = (hits[:, :sub_rows] + hits[:, sub_rows:]).astype(jnp.bfloat16)
+    gate = jnp.sum(hits * gates_row, axis=1, keepdims=True)
+    stacked = jnp.concatenate(
+        [subs[:, h * head_dim : (h + 1) * head_dim] for h in range(heads)], axis=0
+    )
+    send_u[:, :, :head_dim] = (
+        across(pick, stacked, ((1,), (0,))).reshape(owners, capacity, head_dim).astype(jnp.bfloat16)
+    )
+    send_u[:, :, head_dim:] = (
+        jnp.broadcast_to(gate, (slot_count, LANES))
+        .reshape(owners, capacity, LANES)
+        .astype(jnp.bfloat16)
+    )
     for step in range(1, owners):
         t = lax.rem(me + step, owners)
         go(remote(send_u.at[t], recv_u.at[p, me], u_s.at[step], u_r.at[me], t, p))
@@ -305,8 +320,8 @@
         ],
         axis=0,
     )
-    merge_out[...] = across(ordered, tokens, ((0,), (0,))).astype(jnp.bfloat16)
-    stores = [pltpu.make_async_copy(merge_out, merge_any, store_sem.at[0])]
+    ordered_out[...] = ordered
+    stores = [pltpu.make_async_copy(og_buf, tokens_any, store_sem.at[0])]
     stores[0].start()
     from_pair(recv_u, uf_s, uf_r)
     inputs = rows_of(recv_u[:, :, :, :head_dim])
@@ -367,9 +382,11 @@
         sub_out[:, h * head_dim : (h + 1) * head_dim] = gathered[
             h * positions : (h + 1) * positions
         ].astype(jnp.bfloat16)
-    probs_out[...] = across(
-        hits.astype(jnp.bfloat16), returned[:, head_dim:], ((0,), (0,))
-    ).astype(jnp.bfloat16)
+    probs = jnp.sum(hits * returned[:, head_dim:].astype(jnp.float32), axis=0, keepdims=True)
+    for k in range(2):
+        for h in range(heads):
+            at = (k * heads + h) * positions
+            probs_out[h, k : k + 1, :] = probs[:, at : at + positions].astype(jnp.bfloat16)
     for copy in sends:
         copy.wait_send()
     for store in stores:
@@ -388,29 +405,34 @@
     half_cols = wide // d_size
     half_units = expert_in.shape[2]
     padded = head_dim + LANES
-    ids = routes[0].transpose(2, 1, 0).reshape(count)
-    gates = gate_probs[0].transpose(2, 1, 0).reshape(1, count).astype(jnp.float32)
     low = jnp.bfloat16
     dma = pltpu.SemaphoreType.DMA
     vmem = pl.BlockSpec(memory_space=pltpu.VMEM)
     anywhere = pl.BlockSpec(memory_space=pl.ANY)
+    def held(value):
+        return pltpu.with_memory_space_constraint(value, pltpu.HBM)
+
     one, two = dma((owners,)), dma((2 * owners,))
-    merge_grad, grad_sub, probs, grad_in, grad_out = pl.pallas_call(
+    tokens, ordered, grad_sub, probs, grad_in, grad_out = pl.pallas_call(
         functools.partial(layer_kernel, e_size, d_size, capacity, heads),
         out_shape=(
-            jax.ShapeDtypeStruct(merge_weight.shape, low),
+            jax.ShapeDtypeStruct((2, owners, positions, half_cols), low),
+            jax.ShapeDtypeStruct((2 * owners * positions, feats), low),
             jax.ShapeDtypeStruct((positions, wide), low),
-            jax.ShapeDtypeStruct((count, LANES), low),
+            jax.ShapeDtypeStruct((heads, top, positions), low),
             jax.ShapeDtypeStruct((head_dim, half_units), low),
             jax.ShapeDtypeStruct((half_units, head_dim), low),
         ),
-        in_specs=[vmem] * 6 + [anywhere] * 3,
-        out_specs=(anywhere, vmem, vmem, anywhere, anywhere),
+        in_specs=[anywhere] * 4 + [vmem] + [anywhere] * 3,
+        out_specs=(anywhere, vmem, vmem, vmem, anywhere, anywhere),
         scratch_shapes=[
+            pltpu.VMEM((heads, top, positions), jnp.int32),
+            pltpu.VMEM((heads, top, positions), low),
+            pltpu.VMEM((positions, wide), low),
+            pltpu.VMEM((length, feats), low),
             pltpu.VMEM(merge_weight.shape, low),
             pltpu.VMEM((head_dim, half_units), low),
             pltpu.VMEM((half_units, head_dim), low),
-            pltpu.VMEM(merge_weight.shape, low),
             pltpu.VMEM((head_dim, half_units), low),
             pltpu.VMEM((half_units, head_dim), low),
             pltpu.VMEM((2, owners, positions, half_cols), low),
@@ -425,7 +447,7 @@
             pltpu.VMEM((owners, capacity, padded), low),
             pltpu.VMEM((owners, capacity, padded), low),
             pltpu.VMEM((owners, capacity, padded), low),
-            dma((4,)), dma((3,)),
+            dma((8,)), dma((3,)),
             one, one, one, one,
             dma((d_size,)), dma((d_size,)),
             one, one, one, one,
@@ -437,11 +459,14 @@
             collective_id=0, has_side_effects=True, vmem_limit_bytes=48 * 1024 * 1024
         ),
     )(
-        ids.reshape(1, count), ids.reshape(count, 1), gates,
-        out_grad[0], merged[0], sub_tokens[0].reshape(positions, wide),
-        merge_weight, expert_in[0], expert_out[0],
-    )
-    grad_probs = probs[:, 0].reshape(top, heads, positions).transpose(2, 1, 0)
+        held(routes[0].transpose(1, 2, 0)), held(gate_probs[0].transpose(1, 2, 0)),
+        held(out_grad[0]), held(merged[0]), sub_tokens[0].reshape(positions, wide),
+        held(merge_weight), held(expert_in[0]), held(expert_out[0]),
+    )
+    merge_grad = across(
+        ordered, tokens.reshape(2 * owners * positions, half_cols), ((0,), (0,))
+    ).astype(low)
+    grad_probs = probs.transpose(2, 0, 1)
     return (
         merge_grad,
         grad_sub.reshape(sub_tokens.shape),

time: 71.9 us -> 64.4 us (0.90)
  local copies, waits for them, and re-layouts: 13.5 us -> 4.19 us
  matrix products: 0 us -> 2.05 us
    unnamed x14 -> x4, local copies, waits for them, and re-layouts: 11.6 us -> 3.46 us
    dot_general x0 -> x1, matrix products: none -> 2.05 us  [across(): lax.dot_general(left, right, ((dims[0], dims[1]), ((), ())), preferred_el...]
    convert_element_type x2 -> x0, local copies, waits for them, and re-layouts: 0.77 us -> none  [fused(): gate_probs[0].transpose(2, 1, 0).reshape(1, count).astype(jnp.float32)]
where the time goes in v3:
time: 64.4 us; the launch traced here: 63.5 us
  Pallas kernels  56.6 us (88%)
  local copies, waits for them, and re-layouts  4.19 us (7%)
  matrix products  2.05 us (3%)
    pallas_call x1, Pallas kernels, fused(): pl.pallas_call(functools.partial(layer_kernel, e_size, d_size, capacity,...  56.6 us
    unnamed x4, local copies, waits for them, and re-layouts  3.46 us
    dot_general x1, matrix products, across(): lax.dot_general(left, right, ((dims[0], dims[1]), ((), ())), preferred_el...  2.05 us

profile of v3, /device:TPU:0, one launch (start us, length us, event | category | flops | bytes accessed | tf_op | source)
XLA Modules:
  0.0 63.5 jit_solution(9088593752286245922)
XLA Ops:
  0.6 0.9 %copy.22 = bf16[2,8,4,1024]{3,1,2,0:T(8,128)(2,1)S(1)} copy(bf16[2,8,4,1024]{3,2,1,0:T(4,128)(2,1)} %bitcast.30) | data formatting | bytes 262144
  1.6 56.6 %shard_map.119 = (bf16[2,8,16,2048]{3,2,1,0:T(8,128)(2,1)S(1)}, bf16[256,512]{1,0:T(8,128)(2,1)S(1)}, bf16[16,4096]{1,0:T(8,128)(2,1)S(1)}, bf16[4,2,16]{2,1,0:T...) custom-call(s32[4,2,16]{2,1,0:T(2,128)} %bitcast.31, bf16[4,2,16]{2,1,0:T(2,128)(2,1)} %bitcast.32, ...), custom_call_target="tpu_custom_call" | custom-call | tf_op jit(solution)/shard_map/pallas_call | solution.py:416
  58.2 0.7 %reshape.20 = bf16[1,16,4,1024]{3,2,1,0:T(4,128)(2,1)} reshape(bf16[16,4096]{1,0:T(8,128)(2,1)S(1)} %get-tuple-element.13) | data formatting | bytes 262144 | tf_op jit(solution)/shard_map/reshape | solution.py:472
  58.9 2.1 %convolution_convert_fusion = bf16[512,2048]{1,0:T(8,128)(2,1)} fusion(bf16[256,512]{1,0:T(8,128)(2,1)S(1)} %get-tuple-element.11, bf16[256,2048]{1,0:T(8,128)(2,1)S(1)} %bitcast.23), kind=kOutput, calls=%fused_computation | convolution fusion | flops 537919488 | bytes 3407872 | tf_op jit(solution)/shard_map/dot_general | solution.py:133
  60.9 0.6 copy.26
  61.5 1.0 %copy.27 = bf16[1,1024,512]{2,1,0:T(8,128)(2,1)} copy(bf16[1,1024,512]{2,1,0:T(8,128)(2,1)S(1)} %bitcast.22) | data formatting | bytes 2097152
  62.5 1.0 %copy.28 = bf16[1,512,1024]{2,1,0:T(8,128)(2,1)} copy(bf16[1,512,1024]{2,1,0:T(8,128)(2,1)S(1)} %bitcast.21) | data formatting | bytes 2097152

commit v4 on v3

--- a/solution.py
+++ b/solution.py
@@ -141,10 +141,10 @@
     e_size, d_size, capacity, heads,
     ids_any, gates_any, og_any, saved_any, subs, w_any, first_any, second_any,
     tokens_any, ordered_out, sub_out, probs_out, in_any, out_any,
-    ids_in, gates_in, og, saved, w, first, second, in_out, out_out,
+    ids_in, gates_in, og, saved, w, first, second, in_out, out_out, part_own, x_send, x_recv,
     og_buf, saved_buf, send_u, recv_u, send_g, recv_g, part_buf, home_buf, half_buf, pair_buf,
     ret_buf, back_buf,
-    load_sem, store_sem, og_s, og_r, ogf_s, ogf_r, sv_s, sv_r, u_s, u_r, uf_s, uf_r, g_s, g_r, gf_s, gf_r,
+    load_sem, store_sem, x_s, x_r, og_s, og_r, ogf_s, ogf_r, sv_s, sv_r, u_s, u_r, uf_s, uf_r, g_s, g_r, gf_s, gf_r,
     pt_s, pt_r, hf_s, hf_r, rt_s, rt_r,
 ):
     e, d, p = lax.axis_index("expert"), lax.axis_index("dp"), lax.axis_index("pair")
@@ -242,10 +242,9 @@
         .reshape(owners, capacity, LANES)
         .astype(jnp.bfloat16)
     )
-    for step in range(1, owners):
+    for step in range(1, 4):
         t = lax.rem(me + step, owners)
         go(remote(send_u.at[t], recv_u.at[p, me], u_s.at[step], u_r.at[me], t, p))
-    go(remote(send_u.at[me], recv_u.at[p, me], uf_s.at[me], uf_r.at[me], me, other))
     recv_u[p, me] = send_u[me]
 
     def pass_on(buf, recv, fsend, frecv):
@@ -265,29 +264,43 @@
     loads[0].wait()
     from_pair(og_buf, ogf_s, ogf_r)
     tokens = og_buf[...].reshape(2 * owners * positions, half_cols)
-    part_buf[...] = (
-        across(tokens, w[...], ((1,), (1,)))
-        .astype(jnp.bfloat16)
-        .reshape(2, owners, positions, feats)
-    )
-    for step in range(1, 2 * owners):
-        q = lax.rem(mine + step, 2 * owners)
-        t, qp = q // 2, lax.rem(q, 2)
-        go(remote(part_buf.at[qp, t], home_buf.at[p, me], pt_s.at[step], pt_r.at[p, me], t, qp))
-    home_buf[p, me] = part_buf[p, me]
-    for step in range(1, 2 * owners):
-        q = lax.rem(mine + 2 * owners - step, 2 * owners)
-        t, qp = q // 2, lax.rem(q, 2)
+    partial = across(tokens, w[...], ((1,), (1,))).reshape(
+        2 * e_size, d_size, positions, feats
+    )
+    for j in range(d_size):
+        x_send[j] = partial[:, j].astype(jnp.bfloat16)
+        part_own[j] = partial[:, j]
+    for step in range(1, d_size):
+        j = lax.rem(d + step, d_size)
+        go(remote(x_send.at[j], x_recv.at[d], x_s.at[step], x_r.at[d], e * d_size + j, p))
+    for step in range(4, owners):
+        t = lax.rem(me + step, owners)
+        go(remote(send_u.at[t], recv_u.at[p, me], u_s.at[step], u_r.at[me], t, p))
+    go(remote(send_u.at[me], recv_u.at[p, me], uf_s.at[me], uf_r.at[me], me, other))
+    total = part_own[d]
+    for step in range(1, d_size):
+        j = lax.rem(d + d_size - step, d_size)
+        remote(x_recv.at[j], x_recv.at[j], x_s.at[step], x_r.at[j], me, other).wait_recv()
+        total = total + x_recv[j].astype(jnp.float32)
+    part_buf[...] = total.astype(jnp.bfloat16).reshape(2, e_size, positions, feats)
+    spot = e * 2 + p
+    for step in range(1, 2 * e_size):
+        n = lax.rem(spot + step, 2 * e_size)
+        i, q = n // 2, lax.rem(n, 2)
+        go(
+            remote(
+                part_buf.at[q, i], home_buf.at[p, e], pt_s.at[step], pt_r.at[p, e],
+                i * d_size + d, q,
+            )
+        )
+    home_buf[p, e] = part_buf[p, e]
+    for step in range(1, 2 * e_size):
+        n = lax.rem(spot + 2 * e_size - step, 2 * e_size)
+        i, q = n // 2, lax.rem(n, 2)
         remote(
-            home_buf.at[qp, t], home_buf.at[qp, t], pt_s.at[step], pt_r.at[qp, t], me, other
+            home_buf.at[q, i], home_buf.at[q, i], pt_s.at[step], pt_r.at[q, i], me, other
         ).wait_recv()
-    blocks = []
-    for i in range(e_size):
-        for q in range(2):
-            total = home_buf[q, i * d_size].astype(jnp.float32)
-            for j in range(1, d_size):
-                total = total + home_buf[q, i * d_size + j].astype(jnp.float32)
-            blocks.append(total.astype(jnp.bfloat16))
+    blocks = [home_buf[q, i] for i in range(e_size) for q in range(2)]
     per_head = head_dim // feats
     head_rows = jnp.concatenate(
         [
@@ -391,6 +404,32 @@
         copy.wait_send()
     for store in stores:
         store.wait()
+
+
+def finish_kernel(
+    chunk, heads, ordered, tokens, sub, probs_any, in_any, out_any,
+    merge_to, sub_out, probs_to, in_to, out_to, merge_buf, sem, chunk_sem,
+):
+    copies = [
+        pltpu.make_async_copy(in_any, in_to, sem.at[0]),
+        pltpu.make_async_copy(out_any, out_to, sem.at[1]),
+        pltpu.make_async_copy(probs_any, probs_to, sem.at[2]),
+    ]
+    for copy in copies:
+        copy.start()
+    rows = tokens.shape[0] * tokens.shape[1] * tokens.shape[2]
+    for c in range(tokens.shape[3] // chunk):
+        at = pl.ds(c * chunk, chunk)
+        merge_buf[c] = across(
+            ordered[...], tokens[:, :, :, at].reshape(rows, chunk), ((0,), (0,))
+        ).astype(jnp.bfloat16)
+        copies.append(pltpu.make_async_copy(merge_buf.at[c], merge_to.at[:, at], chunk_sem.at[c]))
+        copies[-1].start()
+    width = sub.shape[1] // heads
+    for h in range(heads):
+        sub_out[:, h, :] = sub[:, h * width : (h + 1) * width]
+    for copy in copies:
+        copy.wait()
 
 
 def fused(out_grad, merged, sub_tokens, routes, gate_probs, merge_weight, expert_in, expert_out):
@@ -435,24 +474,27 @@
             pltpu.VMEM((half_units, head_dim), low),
             pltpu.VMEM((head_dim, half_units), low),
             pltpu.VMEM((half_units, head_dim), low),
+            pltpu.VMEM((d_size, 2 * e_size, positions, feats), jnp.float32),
+            pltpu.VMEM((d_size, 2 * e_size, positions, feats), low),
+            pltpu.VMEM((d_size, 2 * e_size, positions, feats), low),
             pltpu.VMEM((2, owners, positions, half_cols), low),
             pltpu.VMEM((d_size, length, feats), low),
             pltpu.VMEM((owners, capacity, padded), low),
             pltpu.VMEM((2, owners, capacity, padded), low),
             pltpu.VMEM((owners, capacity, head_dim), low),
             pltpu.VMEM((2, owners, capacity, head_dim), low),
-            pltpu.VMEM((2, owners, positions, feats), low),
-            pltpu.VMEM((2, owners, positions, feats), low),
+            pltpu.VMEM((2, e_size, positions, feats), low),
+            pltpu.VMEM((2, e_size, positions, feats), low),
             pltpu.VMEM((2, owners, capacity, padded), low),
             pltpu.VMEM((owners, capacity, padded), low),
             pltpu.VMEM((owners, capacity, padded), low),
             pltpu.VMEM((owners, capacity, padded), low),
-            dma((8,)), dma((3,)),
+            dma((8,)), dma((3,)), dma((d_size,)), dma((d_size,)),
             one, one, one, one,
             dma((d_size,)), dma((d_size,)),
             one, one, one, one,
             one, one, one, one,
-            two, dma((2, owners)),
+            two, dma((2, e_size)),
             one, one, one, one,
         ],
         compiler_params=pltpu.CompilerParams(
@@ -463,9 +505,22 @@
         held(out_grad[0]), held(merged[0]), sub_tokens[0].reshape(positions, wide),
         held(merge_weight), held(expert_in[0]), held(expert_out[0]),
     )
-    merge_grad = across(
-        ordered, tokens.reshape(2 * owners * positions, half_cols), ((0,), (0,))
-    ).astype(low)
+    chunk = half_cols // 4
+    shape_of = jax.ShapeDtypeStruct
+    merge_grad, grad_sub, probs, grad_in, grad_out = pl.pallas_call(
+        functools.partial(finish_kernel, chunk, heads),
+        out_shape=(
+            shape_of(merge_weight.shape, low),
+            shape_of((positions, heads, head_dim), low),
+            shape_of(probs.shape, low),
+            shape_of(grad_in.shape, low),
+            shape_of(grad_out.shape, low),
+        ),
+        in_specs=[vmem] * 3 + [anywhere] * 3,
+        out_specs=(anywhere, vmem, anywhere, anywhere, anywhere),
+        scratch_shapes=[pltpu.VMEM((4, feats, chunk), low), dma((3,)), dma((4,))],
+        compiler_params=pltpu.CompilerParams(vmem_limit_bytes=16 * 1024 * 1024),
+    )(ordered, tokens, grad_sub, probs, grad_in, grad_out)
     grad_probs = probs.transpose(2, 0, 1)
     return (
         merge_grad,

time: 64.4 us -> 60.8 us (0.944)
  local copies, waits for them, and re-layouts: 4.19 us -> 0.95 us
  matrix products: 2.05 us -> 0 us
  Pallas kernels: 56.6 us -> 58.4 us
    pallas_call x0 -> x1, Pallas kernels: none -> 2.79 us  [fused(): pl.pallas_call(functools.partial(finish_kernel, chunk, heads), out_shape=...]
    unnamed x4 -> x1, local copies, waits for them, and re-layouts: 3.46 us -> 0.95 us
    dot_general x1 -> x0, matrix products: 2.05 us -> none  [across(): lax.dot_general(left, right, ((dims[0], dims[1]), ((), ())), preferred_el...]
    pallas_call x1, Pallas kernels: 56.6 us -> 55.7 us  [fused(): pl.pallas_call(functools.partial(layer_kernel, e_size, d_size, capacity,...]
    reshape x1 -> x0, local copies, waits for them, and re-layouts: 0.73 us -> none  [fused(): grad_sub.reshape(sub_tokens.shape)]
where the time goes in v4:
time: 60.8 us; the launch traced here: 60 us
  Pallas kernels  58.4 us (96%)
  local copies, waits for them, and re-layouts  0.95 us (2%)
  between operations  0.64 us (1%)
    pallas_call x1, Pallas kernels, fused(): pl.pallas_call(functools.partial(layer_kernel, e_size, d_size, capacity,...  55.7 us
    pallas_call x1, Pallas kernels, fused(): pl.pallas_call(functools.partial(finish_kernel, chunk, heads), out_shape=...  2.79 us

profile of v4, /device:TPU:0, one launch (start us, length us, event | category | flops | bytes accessed | tf_op | source)
XLA Modules:
  0.0 60.0 jit_solution(9201791524926894034)
XLA Ops:
  0.6 0.9 %copy.22 = bf16[2,8,4,1024]{3,1,2,0:T(8,128)(2,1)S(1)} copy(bf16[2,8,4,1024]{3,2,1,0:T(4,128)(2,1)} %bitcast.24) | data formatting | bytes 262144
  1.6 55.7 %shard_map.119 = (bf16[2,8,16,2048]{3,2,1,0:T(8,128)(2,1)S(1)}, bf16[256,512]{1,0:T(8,128)(2,1)S(1)}, bf16[16,4096]{1,0:T(8,128)(2,1)S(1)}, bf16[4,2,16]{2,1,0:T...) custom-call(s32[4,2,16]{2,1,0:T(2,128)} %bitcast.25, bf16[4,2,16]{2,1,0:T(2,128)(2,1)} %bitcast.26, ...), custom_call_target="tpu_custom_call" | custom-call | tf_op jit(solution)/shard_map/pallas_call | solution.py:455
  57.2 2.8 %shard_map.120 = (bf16[512,2048]{1,0:T(8,128)(2,1)}, bf16[16,4,1024]{2,1,0:T(4,128)(2,1)}, bf16[4,2,16]{2,1,0:T(2,128)(2,1)}, bf16[1024,512]{1,0:T(8,128)(2,1)}, bf16[512,1024]{1,0:T(8,128)(2,1)}) custom-call(bf16[256,512]{1,0:T(8,128)(2,1)S(1)} %get-tuple-element.16.ordered, bf16[2,8,16,2048]{3,2,1,0:T(8,128)(2,1)S(1)} %get-tuple-element.17.tokens, ...), custom_call_target="tpu_custom_call" | custom-call | tf_op jit(solution)/shard_map/pallas_call | solution.py:510
